TPU v7x, 768 devices: a whole 4x8x12 slice. The times are simulated.
768 devices in a mesh: loop: 96 (over y, z), group: 8 (over x, core).
Axes of the slice: x: 4, y: 8, z: 12, core: 2. Of those that a mesh axis runs over, the one named last changes fastest.
Arguments:
- images: float32 [49152, 1152], P(('loop', 'group'))
- captions: float32 [49152, 1152], P(('loop', 'group'))
- labels: int32 [49152], P(('loop', 'group')), may hold values from 0 to 49151, as said below
- log_scale: float32 [1], replicated, may hold values from 1 to 2
- logit_bias: float32 [1], replicated, may hold values from -4 to -1
Outputs:
- grad_images: float32 [49152, 1152], P(('loop', 'group'))
- grad_captions: float32 [49152, 1152], P(('loop', 'group'))
Inputs may be any that keep to these rules, and one draw needn't show every extreme that they name: `labels`: the matching text row of an image row in block p lies in block p, p - 1, ..., or p - 2, counted modulo 96.
All inputs are finite; a program needn't handle non-finite values.
Results may differ from a plain program's by a relative error of at most 0.0001.
Values sent between devices are 32-bit elements; how exact they have to be, the bound alone decides.
No kernel may reach another device: no remote copies, remote signals or barrier semaphores. Data moves between devices by JAX's collectives and lax.ppermute only.
A program may use at most 64 MiB of HBM per device.

v0:
```python
import jax
import jax.numpy as jnp
from jax import lax
from jax.sharding import PartitionSpec as P

WIN = 3


EPS = 1e-06


def from_behind(shard, axis, by):
    count = lax.axis_size(axis)
    return lax.ppermute(shard, axis, [(i, (i + by) % count) for i in range(count)])


def normalize(values):
    inverse = lax.rsqrt(jnp.sum(values * values, axis=-1, keepdims=True) + EPS)
    return (values * inverse, inverse)


def unnormalize(unit, inverse, grad_unit):
    along = jnp.sum(unit * grad_unit, axis=-1, keepdims=True)
    return inverse * (grad_unit - unit * along)


def collect(rows):
    return lax.all_gather(rows, "group", axis=0, tiled=True)


def pair_terms(image_unit, block, label_rows, source, temper, offset_bias):
    block_rows = block.shape[0]
    columns = source * block_rows + jnp.arange(block_rows, dtype=jnp.int32)
    positive = (label_rows[:, None] == columns[None, :]).astype(jnp.float32)
    logits = (
        temper
        * lax.dot_general(
            image_unit, block, (((1,), (1,)), ((), ())), precision=lax.Precision.HIGHEST
        )
        + offset_bias
    )
    weights = jax.nn.sigmoid(logits) - positive
    grad_image = temper * jnp.dot(weights, block, precision=lax.Precision.HIGHEST)
    grad_text = temper * lax.dot_general(
        weights, image_unit, (((0,), (0,)), ((), ())), precision=lax.Precision.HIGHEST
    )
    return (grad_image, grad_text)


def per_device(images, captions, labels, log_scale, logit_bias):
    image_unit, image_inverse = normalize(images)
    text_unit, text_inverse = normalize(captions)
    position = lax.axis_index("loop")
    cycle_size = lax.axis_size("loop")
    temper = jnp.exp(log_scale[0])
    offset_bias = logit_bias[0]
    grad_image = jnp.zeros_like(image_unit)
    block = collect(text_unit)
    carried = jnp.zeros_like(block)
    for stride in range(WIN):
        source = (position - stride) % cycle_size
        part_image, part_text = pair_terms(image_unit, block, labels, source, temper, offset_bias)
        grad_image = grad_image + part_image
        carried = carried + part_text
        if stride + 1 < WIN:
            block, carried = from_behind((block, carried), "loop", 1)
    carried = from_behind(carried, "loop", 1 - WIN)
    grad_text = lax.psum_scatter(carried, "group", scatter_dimension=0, tiled=True)
    grad_images = unnormalize(image_unit, image_inverse, grad_image)
    grad_captions = unnormalize(text_unit, text_inverse, grad_text)
    return (grad_images, grad_captions)


def solution(mesh):
    placed = (
        P(("loop", "group"), None),
        P(("loop", "group"), None),
        P(("loop", "group")),
        P(),
        P(),
    )
    return jax.shard_map(
        per_device,
        mesh=mesh,
        in_specs=placed,
        out_specs=(P(("loop", "group"), None), P(("loop", "group"), None)),
        check_vma=False,
    )
```

profile of v0, /device:TPU:1, one launch (start us, length us, event | category | flops | bytes accessed | tf_op | source)
XLA Modules:
  0.0 420.4 jit_solution(16065440370386752947)
XLA Ops:
  7.2 0.0 copy-start
  7.2 0.0 all-gather.2.cloned.1.call-start
  7.2 1.1 multiply_reduce_fusion.2
  8.4 1.8 broadcast_multiply_fusion
  10.1 0.0 all-gather.2.cloned.1.call-update
  10.2 0.0 reduce-scatter.2.cloned.1.call-start
  11.6 1.1 multiply_reduce_fusion.3
  12.7 40.0 %all-gather.2.cloned.1.call-done = f32[512,1152]{1,0:T(8,128)} async-done(((f32[64,1152]{1,0:T(8,128)}), f32[512,1152]{1,0:T(8,128)}) %all-gather.2.cloned.1.call-update) | async-done | bytes 2359312 | tf_op jit(solution)/shard_map/all_gather | solution.py:28
  52.7 3.3 collective-permute-start
  55.9 0.0 copy-start.5
  56.0 4.1 fusion.19
  60.1 0.0 copy-done
  60.1 3.5 convolution_multiply_fusion.2
  63.6 3.3 collective-permute-start.2
  66.9 46.0 %collective-permute-done = f32[512,1152]{1,0:T(8,128)S(1)} collective-permute-done((f32[512,1152]{1,0:T(8,128)}, f32[512,1152]{1,0:T(8,128)S(1)}, u32[]{:S(2)}, u32[]{:S(2)}) %collective-permute-start) | collective-permute-done | bytes 2359328 | tf_op jit(solution)/shard_map/ppermute | solution.py:14
  112.9 0.0 copy-start.2
  112.9 1.9 collective-permute-start.1
  114.8 0.0 copy-done.5
  114.8 2.5 fusion.13
  117.3 46.3 %collective-permute-done.2 = f32[512,1152]{1,0:T(8,128)} collective-permute-done((f32[512,1152]{1,0:T(8,128)}, f32[512,1152]{1,0:T(8,128)}, u32[]{:S(2)}, u32[]{:S(2)}) %collective-permute-start.2) | collective-permute-done | bytes 2359328 | tf_op jit(solution)/shard_map/ppermute | solution.py:14
  163.6 5.1 %fusion = f32[512,1152]{1,0:T(8,128)} fusion(f32[512,1152]{1,0:T(8,128)} %collective-permute-done.2, f32[64,512]{1,0:T(8,128)S(1)} %fusion.13, f32[]{:T(128)} %bitcast, f32[64,1152]{1,0:T(8,128)S(1)} %copy-done, f32[64]{0:T(128)S(1)} %add_rsqrt_fusion.1), kind=kOutput, calls=%fused_computation.3 | convolution fusion | flops 454238208 | bytes 5144836 | tf_op jit(solution)/shard_map/dot_general | solution.py:44
  168.7 0.0 copy-done.2
  168.7 2.1 collective-permute-start.3
  170.8 43.3 %collective-permute-done.1 = f32[512,1152]{1,0:T(8,128)} collective-permute-done((f32[512,1152]{1,0:T(8,128)S(1)}, f32[512,1152]{1,0:T(8,128)}, u32[]{:S(2)}, u32[]{:S(2)}) %collective-permute-start.1) | collective-permute-done | bytes 2359328 | tf_op jit(solution)/shard_map/ppermute | solution.py:14
  214.1 4.1 fusion.7
  218.2 2.1 convolution_multiply_fusion
  220.3 44.4 %collective-permute-done.3 = f32[512,1152]{1,0:T(8,128)} collective-permute-done((f32[512,1152]{1,0:T(8,128)}, f32[512,1152]{1,0:T(8,128)}, u32[]{:S(2)}, u32[]{:S(2)}) %collective-permute-start.3) | collective-permute-done | bytes 2359328 | tf_op jit(solution)/shard_map/ppermute | solution.py:14
  264.7 1.9 add.116
  266.6 0.0 copy-start.1
  266.6 3.9 collective-permute-start.4
  270.5 99.2 %collective-permute-done.4 = f32[512,1152]{1,0:T(8,128)} collective-permute-done((f32[512,1152]{1,0:T(8,128)S(1)}, f32[512,1152]{1,0:T(8,128)}, u32[]{:S(2)}, u32[]{:S(2)}) %collective-permute-start.4) | collective-permute-done | bytes 2359328 | tf_op jit(solution)/shard_map/ppermute | solution.py:14
  369.7 0.0 reduce-scatter.2.cloned.1.call-update
  369.7 0.0 copy-done.1
  369.7 0.0 copy-start.3
  369.7 1.5 fusion.32
  371.2 0.1 copy-done.3
  371.4 1.5 convolution_add_fusion.1
  372.9 0.0 copy-start.4
  372.9 3.3 multiply_reduce_fusion.1
  376.3 0.8 subtract_multiply_fusion.1
  377.1 33.5 %reduce-scatter.2.cloned.1.call-done = f32[64,1152]{1,0:T(8,128)} async-done(((f32[512,1152]{1,0:T(8,128)}), f32[64,1152]{1,0:T(8,128)}) %reduce-scatter.2.cloned.1.call-update) | async-done | bytes 294928 | tf_op jit(solution)/shard_map/reduce_scatter | solution.py:68
  410.6 0.0 copy-done.4
  410.6 1.2 multiply_reduce_fusion
  411.8 1.8 subtract_multiply_fusion
  (5 shorter events, 0.0 us)
Async XLA Ops:
  7.2 52.9 %copy-start = (f32[64,1152]{1,0:T(8,128)S(1)}, f32[64,1152]{1,0:T(8,128)}, u32[]{:S(2)}) copy-start(f32[64,1152]{1,0:T(8,128)} %param.5) | copy-start | bytes 884740
  7.2 45.5 %all-gather.2.cloned.1.call-start = ((), (), s32[]{:S(2)}) async-start(), calls=%async_computation.1 | async-start | bytes 2654208 | tf_op jit(solution)/shard_map/all_gather | solution.py:28
  10.2 400.4 %reduce-scatter.2.cloned.1.call-start = ((), (), s32[]{:S(2)}) async-start(), calls=%async_computation.2 | async-start | bytes 2654208 | tf_op jit(solution)/shard_map/reduce_scatter | solution.py:68
  52.7 60.2 %collective-permute-start = (f32[512,1152]{1,0:T(8,128)}, f32[512,1152]{1,0:T(8,128)S(1)}, u32[]{:S(2)}, u32[]{:S(2)}) collective-permute-start(f32[512,1152]{1,0:T(8,128)} %all-gather.2.cloned.1.call-done), channel_id=1, source_target_pairs={{0,8},{8,16},{16,24},{24,32},{32,40},{40,48},{48,56},{56,64},{64,7... | collective-permute-start | bytes 7077896 | tf_op jit(solution)/shard_map/ppermute | solution.py:14
  55.9 58.9 %copy-start.5 = (s32[64]{0:T(128)S(1)}, s32[64]{0:T(128)}, u32[]{:S(2)}) copy-start(s32[64]{0:T(128)} %param.7) | copy-start | bytes 772
  63.6 100.0 %collective-permute-start.2 = (f32[512,1152]{1,0:T(8,128)}, f32[512,1152]{1,0:T(8,128)}, u32[]{:S(2)}, u32[]{:S(2)}) collective-permute-start(f32[512,1152]{1,0:T(8,128)} %convolution_multiply_fusion.2), channel_id=1, source_target_pairs={{0,8},{8,16},{16,24},{24,32},{32,40},{40,48},{48,56},{56,64},{64,7... | collective-permute-start | bytes 7077896 | tf_op jit(solution)/shard_map/ppermute | solution.py:14
  112.9 55.8 %copy-start.2 = (f32[512,1152]{1,0:T(8,128)}, f32[512,1152]{1,0:T(8,128)S(1)}, u32[]{:S(2)}) copy-start(f32[512,1152]{1,0:T(8,128)S(1)} %collective-permute-done) | copy-start | bytes 7077892
  112.9 101.2 %collective-permute-start.1 = (f32[512,1152]{1,0:T(8,128)S(1)}, f32[512,1152]{1,0:T(8,128)}, u32[]{:S(2)}, u32[]{:S(2)}) collective-permute-start(f32[512,1152]{1,0:T(8,128)S(1)} %collective-permute-done), channel_id=1, source_target_pairs={{0,8},{8,16},{16,24},{24,32},{32,40},{40,48},{48,56},{56,64},{64,7... | collective-permute-start | bytes 7077896 | tf_op jit(solution)/shard_map/ppermute | solution.py:14
  168.7 96.0 %collective-permute-start.3 = (f32[512,1152]{1,0:T(8,128)}, f32[512,1152]{1,0:T(8,128)}, u32[]{:S(2)}, u32[]{:S(2)}) collective-permute-start(f32[512,1152]{1,0:T(8,128)} %fusion), channel_id=1, source_target_pairs={{0,8},{8,16},{16,24},{24,32},{32,40},{40,48},{48,56},{56,64},{64,7... | collective-permute-start | bytes 7077896 | tf_op jit(solution)/shard_map/ppermute | solution.py:14
  266.6 103.1 %copy-start.1 = (f32[512,1152]{1,0:T(8,128)S(1)}, f32[512,1152]{1,0:T(8,128)}, u32[]{:S(2)}) copy-start(f32[512,1152]{1,0:T(8,128)} %all-gather.2.cloned.1.call-done) | copy-start | bytes 7077892
  266.6 103.1 %collective-permute-start.4 = (f32[512,1152]{1,0:T(8,128)S(1)}, f32[512,1152]{1,0:T(8,128)}, u32[]{:S(2)}, u32[]{:S(2)}) collective-permute-start(f32[512,1152]{1,0:T(8,128)S(1)} %add.116), channel_id=1, source_target_pairs={{0,752},{8,760},{16,0},{24,8},{32,16},{40,24},{48,32},{56,40},{64,... | collective-permute-start | bytes 7077896 | tf_op jit(solution)/shard_map/ppermute | solution.py:14
  369.7 1.7 copy-start.3
  372.9 37.7 %copy-start.4 = (f32[64,1152]{1,0:T(8,128)S(1)}, f32[64,1152]{1,0:T(8,128)}, u32[]{:S(2)}) copy-start(f32[64,1152]{1,0:T(8,128)} %param.6) | copy-start | bytes 884740
Sparse Core Ops, SparseCore 0:
  11.0 41.6 all-gather.1
  369.8 40.7 reduce-scatter.1
where the time goes:
time: 421 us; the launch traced here: 420 us
  waiting for transfers between devices  353 us (84%)
  matrix products  27.7 us (7%)
  between operations  15.6 us (4%)
  starting transfers between devices  14.5 us (3%)
  other arithmetic  9.7 us (2%)
    ppermute x5, waiting for transfers between devices, from_behind(): lax.ppermute(shard, axis, [(i, (i + by) % count) for i in range(count)])  279 us
    all_gather x1, waiting for transfers between devices, collect(): return lax.all_gather(rows, 'group', axis=0, tiled=True)  40 us
    reduce_scatter x1, waiting for transfers between devices, per_device(): lax.psum_scatter(carried, 'group', scatter_dimension=0, tiled=True)  33.5 us
    ppermute x5, starting transfers between devices, from_behind(): lax.ppermute(shard, axis, [(i, (i + by) % count) for i in range(count)])  14.4 us
    dot_general x3, matrix products, pair_terms(): lax.dot_general(image_unit, block, (((1,), (1,)), ((), ())), precision=la...  10.7 us
    dot_general x3, matrix products, pair_terms(): lax.dot_general(weights, image_unit, (((0,), (0,)), ((), ())), precision=...  10.7 us
  transfers between devices with their start and end apart: 7, of which 7 were waited for; matrix products, arithmetic and copies ran while one was open for 7% of the time, Pallas kernels for 0%

commit v1 on v0

v1 whole, which is shorter than its diff:
```python
import jax
import jax.numpy as jnp
from jax import lax
from jax.experimental import pallas as pl
from jax.experimental.pallas import tpu as pltpu
from jax.sharding import PartitionSpec as P

WIN = 3
ROWS = 64
PACK = 72
D = 1152
X = 4
EPS = 1e-06
VMEM_LIMIT = 12 * 1024 * 1024


def along_loop(shard, by):
    count = lax.axis_size("loop")
    return lax.ppermute(shard, "loop", [(i, (i + by) % count) for i in range(count)])


def along_x(shard, by):
    count = lax.axis_size("group")
    return lax.ppermute(shard, "group", [(i, (i + 2 * by) % count) for i in range(count)])


def across_cores(shard):
    count = lax.axis_size("group")
    return lax.ppermute(shard, "group", [(i, i ^ 1) for i in range(count)])


def split(values):
    high = values.astype(jnp.bfloat16)
    low = (values - high.astype(jnp.float32)).astype(jnp.bfloat16)
    return high, low


NT = (((1,), (1,)), ((), ()))
NN = (((1,), (0,)), ((), ()))
TN = (((0,), (0,)), ((), ()))


def dot3(a, b, dims):
    def one(left, right):
        return lax.dot_general(left, right, dims, preferred_element_type=jnp.float32)

    return one(a[0], b[0]) + (one(a[0], b[1]) + one(a[1], b[0]))


def unit_rows(values):
    return values * lax.rsqrt(jnp.sum(values * values, axis=-1, keepdims=True) + EPS)


def label_row(packs):
    width = X * ROWS
    lane = lax.broadcasted_iota(jnp.int32, (1, width), 1)
    rows = [pack[ROWS : ROWS + 1, :width] for pack in packs]
    result = rows[X - 1]
    for k in range(X - 2, -1, -1):
        result = jnp.where(lane < (k + 1) * ROWS, rows[k], result)
    return result


def weights(texts, images, labels, scalars, base):
    def value(at):
        return scalars[at : at + 1, 0:1]

    sums = dot3(texts, images, NT)
    logits = value(0) * sums + value(1)
    row = lax.broadcasted_iota(jnp.int32, (WIN * ROWS, 1), 0)
    offset = jnp.where(
        row < ROWS,
        value(base),
        jnp.where(row < 2 * ROWS, value(base + 1) - ROWS, value(base + 2) - 2 * ROWS),
    )
    index = row.astype(jnp.float32) + offset
    positive = (index == labels).astype(jnp.float32)
    return split(jax.nn.sigmoid(logits) - positive)


def pack_kernel(images, labels, out, row, sem):
    images_in = pltpu.make_async_copy(images, out.at[pl.ds(0, ROWS), :], sem.at[0])
    label_in = pltpu.make_async_copy(labels, row, sem.at[1])
    images_in.start()
    label_in.start()
    label_in.wait()
    wide = row[...].astype(jnp.float32)
    wide = jnp.concatenate([wide, wide], axis=1)
    wide = jnp.concatenate([wide] * (D // (2 * ROWS)), axis=1)
    out[ROWS:, :] = jnp.broadcast_to(wide, (PACK - ROWS, D))
    images_in.wait()


def early_kernel(log_scale, logit_bias, places, t0, t1, scalars, units, t_high, t_low):
    for k, text in enumerate((t0, t1)):
        for r in range(0, ROWS, 32):
            at = k * ROWS + r
            unit = unit_rows(text[r : r + 32, :])
            units[at : at + 32, :] = unit
            t_high[at : at + 32, :], t_low[at : at + 32, :] = split(unit)

    def wide(value):
        return jnp.broadcast_to(value, (1, scalars.shape[1]))

    scalars[0:1, :] = jnp.exp(wide(log_scale[...]))
    scalars[1:2, :] = wide(logit_bias[...])
    for k in range(2 * WIN):
        scalars[2 + k : 3 + k, :] = wide(places[0:1, k : k + 1])


def late_kernel(t2, early_units, early_high, early_low, units, t_high, t_low):
    early = 2 * ROWS
    units[:early, :] = early_units[...]
    t_high[:early, :] = early_high[...]
    t_low[:early, :] = early_low[...]
    for r in range(0, ROWS, 32):
        at = early + r
        unit = unit_rows(t2[r : r + 32, :])
        units[at : at + 32, :] = unit
        t_high[at : at + 32, :], t_low[at : at + 32, :] = split(unit)


def own_kernel(
    scalars, p0, p1, p2, p3, t_high, t_low, x_high, x_low, labels, w_high, w_low, grad_text
):
    packs = (p0, p1, p2, p3)
    for k, pack in enumerate(packs):
        for r in range(0, ROWS, 32):
            at = k * ROWS + r
            x_high[at : at + 32, :], x_low[at : at + 32, :] = split(
                unit_rows(pack[r : r + 32, :])
            )
    row = label_row(packs)
    labels[...] = jnp.broadcast_to(row, labels.shape)
    images = (x_high[...], x_low[...])
    weight = weights((t_high[...], t_low[...]), images, row, scalars, 2)
    w_high[...], w_low[...] = weight
    grad_text[...] = dot3(weight, images, NN)


def cross_kernel(
    scalars, units, x_high, x_low, labels, t_high, t_low, w_high, w_low, grad_text
):
    for at in range(0, WIN * ROWS, 32):
        t_high[at : at + 32, :], t_low[at : at + 32, :] = split(units[at : at + 32, :])
    images = (x_high[...], x_low[...])
    weight = weights((t_high[...], t_low[...]), images, labels[0:1, :], scalars, 5)
    w_high[...], w_low[...] = weight
    grad_text[...] = dot3(weight, images, NN)


def image_kernel(
    w_high, w_low, t_high, t_low, ow_high, ow_low, ot_high, ot_low, o0, o1, o2, o3
):
    total = dot3((w_high[...], w_low[...]), (t_high[...], t_low[...]), TN) + dot3(
        (ow_high[...], ow_low[...]), (ot_high[...], ot_low[...]), TN
    )
    for k, out in enumerate((o0, o1, o2, o3)):
        out[...] = total[k * ROWS : (k + 1) * ROWS, :]


def last_kernel(own, other, after, out):
    at = (WIN - 1) * ROWS
    out[...] = own[at:, :] + other[at:, :]


def middle_kernel(own, other, back, out):
    out[...] = (own[ROWS : 2 * ROWS, :] + other[ROWS : 2 * ROWS, :]) + back[...]


def finish(values, grad, temper):
    inverse = lax.rsqrt(jnp.sum(values * values, axis=-1, keepdims=True) + EPS)
    unit = values * inverse
    grad = temper * grad
    along = jnp.sum(unit * grad, axis=-1, keepdims=True)
    return inverse * (grad - unit * along)


def final_kernel(
    scalars, images, captions, i0, i1, i2, i3, own, other, back, out_images, out_captions
):
    temper = scalars[0:1, 0:1]
    for r in range(0, ROWS, 32):
        at = slice(r, r + 32)
        grad = (own[at, :] + other[at, :]) + back[at, :]
        out_captions[at, :] = finish(captions[at, :], grad, temper)
        grad = (i0[at, :] + i1[at, :]) + (i2[at, :] + i3[at, :])
        out_images[at, :] = finish(images[at, :], grad, temper)


VMEM = pl.BlockSpec(memory_space=pltpu.VMEM)
HBM = pl.BlockSpec(memory_space=pl.ANY)


def f32(*shape):
    return jax.ShapeDtypeStruct(shape, jnp.float32)


def b16(*shape):
    return jax.ShapeDtypeStruct(shape, jnp.bfloat16)


def call(kernel, inputs, outs, products):
    return pl.pallas_call(
        kernel,
        in_specs=[VMEM] * inputs,
        out_specs=[VMEM] * len(outs),
        out_shape=outs,
        compiler_params=pltpu.CompilerParams(vmem_limit_bytes=VMEM_LIMIT),
        cost_estimate=pl.CostEstimate(
            flops=products * 3 * 2 * X * ROWS * WIN * ROWS * D,
            bytes_accessed=6 * X * ROWS * D * 4,
            transcendentals=X * ROWS * WIN * ROWS,
        ),
        name=kernel.__name__,
    )


def per_device(images, captions, labels, log_scale, logit_bias):
    position = lax.axis_index("loop")
    cycle_size = lax.axis_size("loop")
    member = lax.axis_index("group")
    members = lax.axis_size("group")
    images_all = X * ROWS
    texts_all = WIN * ROWS
    image_halves = [b16(images_all, D)] * 2
    text_halves = [b16(texts_all, D)] * 2

    text1 = along_loop(captions, 1)
    text2 = along_loop(text1, 1)
    pack = pl.pallas_call(
        pack_kernel,
        in_specs=[HBM, HBM],
        out_specs=VMEM,
        out_shape=f32(PACK, D),
        scratch_shapes=[pltpu.VMEM((1, ROWS), jnp.int32), pltpu.SemaphoreType.DMA((2,))],
        compiler_params=pltpu.CompilerParams(vmem_limit_bytes=VMEM_LIMIT),
        name="pack_kernel",
    )(images, labels[None, :])
    pack2, pack1, pack3 = (along_x(pack, k) for k in (2, 1, 3))

    places = []
    for who in (member, member ^ 1):
        for stride in range(WIN):
            source = (position - stride) % cycle_size
            places.append(source * (members * ROWS) + who * ROWS)
    places = jnp.stack(places).astype(jnp.float32)[None, :]
    scalars, *early = call(
        early_kernel, 5, [f32(8, 128), f32(2 * ROWS, D)] + [b16(2 * ROWS, D)] * 2, 60
    )(log_scale[None, :], logit_bias[None, :], places, captions, text1)
    units, t_high, t_low = call(late_kernel, 4, [f32(texts_all, D)] + text_halves, 0)(
        text2, *early
    )
    other_units = across_cores(units)

    weight_halves = [b16(texts_all, images_all)] * 2
    x_high, x_low, label_rows, w_high, w_low, own_text = call(
        own_kernel,
        7,
        image_halves + [f32(8, images_all)] + weight_halves + [f32(texts_all, D)],
        60,
    )(scalars, pack, pack1, pack2, pack3, t_high, t_low)
    ot_high, ot_low, ow_high, ow_low, other_text = call(
        cross_kernel, 5, text_halves + weight_halves + [f32(texts_all, D)], 2
    )(scalars, other_units, x_high, x_low, label_rows)
    other_text = across_cores(other_text)
    i0, i1, i2, i3 = call(image_kernel, 8, [f32(ROWS, D)] * X, 2)(
        w_high, w_low, t_high, t_low, ow_high, ow_low, ot_high, ot_low
    )
    back = pl.pallas_call(
        last_kernel,
        in_specs=[VMEM, VMEM, HBM],
        out_specs=VMEM,
        out_shape=f32(ROWS, D),
        compiler_params=pltpu.CompilerParams(vmem_limit_bytes=VMEM_LIMIT),
        name="last_kernel",
    )(own_text, other_text, i0)
    back = along_loop(back, -1)
    (back,) = call(middle_kernel, 3, [f32(ROWS, D)], 0)(own_text, other_text, back)
    back = along_loop(back, -1)
    i2, i1, i3 = along_x(i2, -2), along_x(i1, -1), along_x(i3, -3)

    first = pl.BlockSpec((ROWS, D), lambda i: (0, 0))
    return tuple(
        pl.pallas_call(
            final_kernel,
            grid=(1,),
            in_specs=[pl.BlockSpec((8, 128), lambda i: (0, 0))] + [first] * 9,
            out_specs=[first] * 2,
            out_shape=[f32(ROWS, D)] * 2,
            compiler_params=pltpu.CompilerParams(vmem_limit_bytes=VMEM_LIMIT),
            name="finish",
        )(scalars, images, captions, i0, i2, i1, i3, own_text, other_text, back)
    )


def solution(mesh):
    rows = P(("loop", "group"), None)
    placed = (rows, rows, P(("loop", "group")), P(), P())
    return jax.shard_map(
        per_device, mesh=mesh, in_specs=placed, out_specs=(rows, rows), check_vma=False
    )
```

time: 421 us -> 75.9 us (0.18)
  waiting for transfers between devices: 353 us -> 24.9 us
  matrix products: 27.7 us -> 0 us
  starting transfers between devices: 14.5 us -> 39.5 us
  between operations: 15.6 us -> 2.21 us
  other arithmetic: 9.7 us -> 0.01 us
  Pallas kernels: 0 us -> 7.04 us
    ppermute x5 -> x12, waiting for transfers between devices: 279 us -> 24.9 us  [the longest x4 19.6 us: along_loop(): lax.ppermute(shard, 'loop', [(i, (i + by) % count) for i in range(count)])]
    all_gather x1 -> x0, waiting for transfers between devices: 40 us -> none  [collect(): return lax.all_gather(rows, 'group', axis=0, tiled=True)]
    reduce_scatter x1 -> x0, waiting for transfers between devices: 33.5 us -> none  [per_device(): lax.psum_scatter(carried, 'group', scatter_dimension=0, tiled=True)]
    dot_general x9 -> x0, matrix products: 27.7 us -> none  [the longest x3 10.7 us: pair_terms(): lax.dot_general(image_unit, block, (((1,), (1,)), ((), ())), precision=la...]
    ppermute x5 -> x12, starting transfers between devices: 14.4 us -> 39.5 us  [the longest x6 18.6 us: along_x(): lax.ppermute(shard, 'group', [(i, (i + 2 * by) % count) for i in range(co...]
    pallas_call x0 -> x9, Pallas kernels: none -> 7.04 us  [the longest x1 2.13 us: per_device(): call(own_kernel, 7, image_halves + [f32(8, images_all)] + weight_halves +...]
    mul x3 -> x0, other arithmetic: 4.41 us -> none  [the longest x2 2.64 us: unnormalize(): return inverse * (grad_unit - unit * along)]
  transfers between devices with their start and end apart: 7 -> 12, of which waited for: 7 -> 6; matrix products, arithmetic and copies ran while one was open for 7% -> 0% of each run, Pallas kernels for 0% -> 5%
where the time goes in v1:
time: 75.9 us; the launch traced here: 74.8 us
  starting transfers between devices  39.5 us (52%)
  waiting for transfers between devices  24.9 us (33%)
  Pallas kernels  7.04 us (9%)
  between operations  2.21 us (3%)
  local copies, waits for them, and re-layouts  1.07 us (1%)
    ppermute x4, waiting for transfers between devices, along_loop(): lax.ppermute(shard, 'loop', [(i, (i + by) % count) for i in range(count)])  19.6 us
    ppermute x6, starting transfers between devices, along_x(): lax.ppermute(shard, 'group', [(i, (i + 2 * by) % count) for i in range(co...  18.6 us
    ppermute x4, starting transfers between devices, along_loop(): lax.ppermute(shard, 'loop', [(i, (i + by) % count) for i in range(count)])  14.7 us
    ppermute x2, starting transfers between devices, across_cores(): return lax.ppermute(shard, 'group', [(i, i ^ 1) for i in range(count)])  6.2 us
    ppermute x6, waiting for transfers between devices, along_x(): lax.ppermute(shard, 'group', [(i, (i + 2 * by) % count) for i in range(co...  4.44 us
    pallas_call x1, Pallas kernels, per_device(): call(own_kernel, 7, image_halves + [f32(8, images_all)] + weight_halves +...  2.13 us
    pallas_call x1, Pallas kernels, per_device(): call(cross_kernel, 5, text_halves + weight_halves + [f32(texts_all, D)], 2)  1.96 us
  transfers between devices with their start and end apart: 12, of which 6 were waited for; matrix products, arithmetic and copies ran while one was open for 0% of the time, Pallas kernels for 5%

profile of v1, /device:TPU:1, one launch (start us, length us, event | category | flops | bytes accessed | tf_op | source)
XLA Modules:
  0.0 74.8 jit_solution(16722559621165170708)
XLA Ops:
  0.6 0.0 copy-start.3
  0.6 4.8 %collective-permute-start = (f32[64,1152]{1,0:T(8,128)}, f32[64,1152]{1,0:T(8,128)S(1)}, u32[]{:S(2)}, u32[]{:S(2)}) collective-permute-start(f32[64,1152]{1,0:T(8,128)} %captions.1), channel_id=1, source_target_pairs={{0,8},{8,16},{16,24},{24,32},{32,40},{40,48},{48,56},{56,64},{64,7... | collective-permute-start | bytes 884744 | tf_op jit(solution)/shard_map/ppermute | solution.py:19
  5.5 0.0 copy-done.3
  5.5 0.0 copy-start
  5.5 1.0 %copy-done = f32[64,1152]{1,0:T(8,128)S(1)} copy-done((f32[64,1152]{1,0:T(8,128)S(1)}, f32[64,1152]{1,0:T(8,128)}, u32[]{:S(2)}) %copy-start) | copy-done | bytes 294936
  6.5 0.0 copy-start.2
  6.5 0.2 pack_kernel.1.p0
  6.6 4.4 %collective-permute-start.3 = (f32[72,1152]{1,0:T(8,128)S(1)}, f32[72,1152]{1,0:T(8,128)S(1)}, u32[]{:S(2)}, u32[]{:S(2)}) collective-permute-start(f32[72,1152]{1,0:T(8,128)S(1)} %pack_kernel.1.p0), channel_id=1, source_target_pairs={{0,6},{1,7},{2,0},{3,1},{4,2},{5,3},{6,4},{7,5},{8,14},{9,15},{10,... | collective-permute-start | bytes 995336 | tf_op jit(solution)/shard_map/ppermute | solution.py:24
  11.0 2.4 %collective-permute-start.2 = (f32[72,1152]{1,0:T(8,128)S(1)}, f32[72,1152]{1,0:T(8,128)S(1)}, u32[]{:S(2)}, u32[]{:S(2)}) collective-permute-start(f32[72,1152]{1,0:T(8,128)S(1)} %pack_kernel.1.p0), channel_id=1, source_target_pairs={{0,4},{1,5},{2,6},{3,7},{4,0},{5,1},{6,2},{7,3},{8,12},{9,13},{10,... | collective-permute-start | bytes 995336 | tf_op jit(solution)/shard_map/ppermute | solution.py:24
  13.4 2.5 %collective-permute-start.1 = (f32[72,1152]{1,0:T(8,128)S(1)}, f32[72,1152]{1,0:T(8,128)S(1)}, u32[]{:S(2)}, u32[]{:S(2)}) collective-permute-start(f32[72,1152]{1,0:T(8,128)S(1)} %pack_kernel.1.p0), channel_id=1, source_target_pairs={{0,2},{1,3},{2,4},{3,5},{4,6},{5,7},{6,0},{7,1},{8,10},{9,11},{10,... | collective-permute-start | bytes 995336 | tf_op jit(solution)/shard_map/ppermute | solution.py:24
  17.3 0.1 stack.27
  17.4 8.2 %collective-permute-done.t1 = f32[64,1152]{1,0:T(8,128)S(1)} collective-permute-done((f32[64,1152]{1,0:T(8,128)}, f32[64,1152]{1,0:T(8,128)S(1)}, u32[]{:S(2)}, u32[]{:S(2)}) %collective-permute-start) | collective-permute-done | bytes 294944 | tf_op jit(solution)/shard_map/ppermute | solution.py:19
  25.6 1.9 %collective-permute-start.4 = (f32[64,1152]{1,0:T(8,128)S(1)}, f32[64,1152]{1,0:T(8,128)S(1)}, u32[]{:S(2)}, u32[]{:S(2)}) collective-permute-start(f32[64,1152]{1,0:T(8,128)S(1)} %collective-permute-done.t1), channel_id=1, source_target_pairs={{0,8},{8,16},{16,24},{24,32},{32,40},{40,48},{48,56},{56,64},{64,7... | collective-permute-start | bytes 884744 | tf_op jit(solution)/shard_map/ppermute | solution.py:19
  27.5 0.0 copy-done.2
  27.5 0.2 early_kernel.1
  27.8 10.6 %collective-permute-done.4.t2 = f32[64,1152]{1,0:T(8,128)S(1)} collective-permute-done((f32[64,1152]{1,0:T(8,128)S(1)}, f32[64,1152]{1,0:T(8,128)S(1)}, u32[]{:S(2)}, u32[]{:S(2)}) %collective-permute-start.4) | collective-permute-done | bytes 294944 | tf_op jit(solution)/shard_map/ppermute | solution.py:19
  38.4 0.2 late_kernel.1
  38.5 4.1 %collective-permute-start.5 = (f32[192,1152]{1,0:T(8,128)S(1)}, f32[192,1152]{1,0:T(8,128)S(1)}, u32[]{:S(2)}, u32[]{:S(2)}) collective-permute-start(f32[192,1152]{1,0:T(8,128)S(1)} %get-tuple-element.32), channel_id=1, source_target_pairs={{0,1},{1,0},{2,3},{3,2},{4,5},{5,4},{6,7},{7,6},{8,9},{9,8},{10,11... | collective-permute-start | bytes 2654216 | tf_op jit(solution)/shard_map/ppermute | solution.py:29
  42.6 0.0 collective-permute-done.3.p3
  42.6 0.0 collective-permute-done.2.p2
  42.6 0.0 collective-permute-done.1.p1
  42.6 2.1 %own_kernel.1 = (bf16[256,1152]{1,0:T(8,128)(2,1)S(1)}, bf16[256,1152]{1,0:T(8,128)(2,1)S(1)}, f32[8,256]{1,0:T(8,128)S(1)}, bf16[192,256]{1,0:T(8,128)(2,1)S(1)...) custom-call(f32[8,128]{1,0:T(8,128)S(1)} %get-tuple-element.24.scalars, f32[72,1152]{1,0:T(8,128)S(1)} %pack_kernel.1.p0, ...), custom_call_target="tpu_custom_call" | custom-call | flops 20384317440 | bytes 7077888 | tf_op jit(solution)/shard_map/own_kernel/pallas_call | solution.py:257
  44.8 0.0 collective-permute-done.5.units
  44.8 2.0 %cross_kernel.1 = (bf16[192,1152]{1,0:T(8,128)(2,1)S(1)}, bf16[192,1152]{1,0:T(8,128)(2,1)S(1)}, bf16[192,256]{1,0:T(8,128)(2,1)S(1)}, bf16[192,256]{1,0:T(8,128)(2,1)S(1)}, f32[192,1152]{1,0:T(8,128)S(1)}) custom-call(f32[8,128]{1,0:T(8,128)S(1)} %get-tuple-element.24.scalars, f32[192,1152]{1,0:T(8,128)S(1)} %collective-permute-done.5.units, ...), custom_call_target="tpu_custom_call" | custom-call | flops 679477248 | bytes 7077888 | tf_op jit(solution)/shard_map/cross_kernel/pallas_call | solution.py:263
  46.7 2.1 %collective-permute-start.9 = (f32[192,1152]{1,0:T(8,128)S(1)}, f32[192,1152]{1,0:T(8,128)S(1)}, u32[]{:S(2)}, u32[]{:S(2)}) collective-permute-start(f32[192,1152]{1,0:T(8,128)S(1)} %get-tuple-element.45), channel_id=1, source_target_pairs={{0,1},{1,0},{2,3},{3,2},{4,5},{5,4},{6,7},{7,6},{8,9},{9,8},{10,11... | collective-permute-start | bytes 2654216 | tf_op jit(solution)/shard_map/ppermute | solution.py:29
  48.9 1.2 %image_kernel.1 = (f32[64,1152]{1,0:T(8,128)S(1)}, f32[64,1152]{1,0:T(8,128)S(1)}, f32[64,1152]{1,0:T(8,128)S(1)}, f32[64,1152]{1,0:T(8,128)S(1)}) custom-call(bf16[192,256]{1,0:T(8,128)(2,1)S(1)} %get-tuple-element.30.w_high, bf16[192,256]{1,0:T(8,128)(2,1)S(1)} %get-tuple-element.31.w_low, bf16[192,1152]{1,0:T(8,128)(2,1)S(1)} %get-tuple-element.28.t_high, ...), custom_call_target="tpu_custom_call" | custom-call | flops 679477248 | bytes 7077888 | tf_op jit(solution)/shard_map/image_kernel/pallas_call | solution.py:267
  50.1 0.9 %collective-permute-done.9.other = f32[192,1152]{1,0:T(8,128)S(1)} collective-permute-done((f32[192,1152]{1,0:T(8,128)S(1)}, f32[192,1152]{1,0:T(8,128)S(1)}, u32[]{:S(2)}, u32[]{:S(2)}) %collective-permute-start.9) | collective-permute-done | bytes 884768 | tf_op jit(solution)/shard_map/ppermute | solution.py:29
  51.1 3.9 %collective-permute-start.10 = (f32[64,1152]{1,0:T(8,128)S(1)}, f32[64,1152]{1,0:T(8,128)S(1)}, u32[]{:S(2)}, u32[]{:S(2)}) collective-permute-start(f32[64,1152]{1,0:T(8,128)S(1)} %last_kernel.1), channel_id=1, source_target_pairs={{0,760},{8,0},{16,8},{24,16},{32,24},{40,32},{48,40},{56,48},{64,5... | collective-permute-start | bytes 884744 | tf_op jit(solution)/shard_map/ppermute | solution.py:19
  55.0 3.3 %collective-permute-start.6 = (f32[64,1152]{1,0:T(8,128)S(1)}, f32[64,1152]{1,0:T(8,128)S(1)}, u32[]{:S(2)}, u32[]{:S(2)}) collective-permute-start(f32[64,1152]{1,0:T(8,128)S(1)} %get-tuple-element.41), channel_id=1, source_target_pairs={{0,4},{1,5},{2,6},{3,7},{4,0},{5,1},{6,2},{7,3},{8,12},{9,13},{10,... | collective-permute-start | bytes 884744 | tf_op jit(solution)/shard_map/ppermute | solution.py:24
  58.2 4.0 %collective-permute-start.7 = (f32[64,1152]{1,0:T(8,128)S(1)}, f32[64,1152]{1,0:T(8,128)S(1)}, u32[]{:S(2)}, u32[]{:S(2)}) collective-permute-start(f32[64,1152]{1,0:T(8,128)S(1)} %get-tuple-element.42), channel_id=1, source_target_pairs={{0,6},{1,7},{2,0},{3,1},{4,2},{5,3},{6,4},{7,5},{8,14},{9,15},{10,... | collective-permute-start | bytes 884744 | tf_op jit(solution)/shard_map/ppermute | solution.py:24
  62.2 0.0 copy-start.1
  62.2 2.1 %collective-permute-start.8 = (f32[64,1152]{1,0:T(8,128)S(1)}, f32[64,1152]{1,0:T(8,128)S(1)}, u32[]{:S(2)}, u32[]{:S(2)}) collective-permute-start(f32[64,1152]{1,0:T(8,128)S(1)} %get-tuple-element.43), channel_id=1, source_target_pairs={{0,2},{1,3},{2,4},{3,5},{4,6},{5,7},{6,0},{7,1},{8,10},{9,11},{10,... | collective-permute-start | bytes 884744 | tf_op jit(solution)/shard_map/ppermute | solution.py:24
  64.3 0.0 collective-permute-done.10.back
  64.3 0.1 middle_kernel.1
  64.4 4.1 %collective-permute-start.11 = (f32[64,1152]{1,0:T(8,128)S(1)}, f32[64,1152]{1,0:T(8,128)S(1)}, u32[]{:S(2)}, u32[]{:S(2)}) collective-permute-start(f32[64,1152]{1,0:T(8,128)S(1)} %middle_kernel.1), channel_id=1, source_target_pairs={{0,760},{8,0},{16,8},{24,16},{32,24},{40,32},{48,40},{56,48},{64,5... | collective-permute-start | bytes 884744 | tf_op jit(solution)/shard_map/ppermute | solution.py:19
  68.5 0.0 collective-permute-done.6.i1
  68.5 3.5 %collective-permute-done.7.i2 = f32[64,1152]{1,0:T(8,128)S(1)} collective-permute-done((f32[64,1152]{1,0:T(8,128)S(1)}, f32[64,1152]{1,0:T(8,128)S(1)}, u32[]{:S(2)}, u32[]{:S(2)}) %collective-permute-start.7) | collective-permute-done | bytes 294944 | tf_op jit(solution)/shard_map/ppermute | solution.py:24
  72.0 0.9 %collective-permute-done.8.i3 = f32[64,1152]{1,0:T(8,128)S(1)} collective-permute-done((f32[64,1152]{1,0:T(8,128)S(1)}, f32[64,1152]{1,0:T(8,128)S(1)}, u32[]{:S(2)}, u32[]{:S(2)}) %collective-permute-start.8) | collective-permute-done | bytes 294944 | tf_op jit(solution)/shard_map/ppermute | solution.py:24
  72.9 0.8 %collective-permute-done.11.back = f32[64,1152]{1,0:T(8,128)S(1)} collective-permute-done((f32[64,1152]{1,0:T(8,128)S(1)}, f32[64,1152]{1,0:T(8,128)S(1)}, u32[]{:S(2)}, u32[]{:S(2)}) %collective-permute-start.11) | collective-permute-done | bytes 294944 | tf_op jit(solution)/shard_map/ppermute | solution.py:19
  73.7 0.0 copy-done.1
  73.7 1.1 %finish.1 = (f32[64,1152]{1,0:T(8,128)}, f32[64,1152]{1,0:T(8,128)}) custom-call(f32[8,128]{1,0:T(8,128)S(1)} %get-tuple-element.24.scalars, f32[64,1152]{1,0:T(8,128)S(1)} %copy-done.1, f32[64,1152]{1,0:T(8,128)S(1)} %copy-done.2, f32[64,1152]{1,0:T(8,128)S(1)} %get-tuple-element.40.after.i0, f32[64,1152]{1,0:T(8,128)S(1)} %collective-permute-done.6.i1, ...), custom_call_target="tpu_custom_call" | custom-call | tf_op jit(solution)/shard_map/finish/pallas_call | solution.py:285
  (2 shorter events, 0.0 us)
Async XLA Ops:
  0.6 4.8 %copy-start.3 = (s32[64]{0:T(128)S(1)}, s32[64]{0:T(128)}, u32[]{:S(2)}) copy-start(s32[64]{0:T(128)} %param.7) | copy-start | bytes 772
  0.6 25.0 %collective-permute-start = (f32[64,1152]{1,0:T(8,128)}, f32[64,1152]{1,0:T(8,128)S(1)}, u32[]{:S(2)}, u32[]{:S(2)}) collective-permute-start(f32[64,1152]{1,0:T(8,128)} %captions.1), channel_id=1, source_target_pairs={{0,8},{8,16},{16,24},{24,32},{32,40},{40,48},{48,56},{56,64},{64,7... | collective-permute-start | bytes 884744 | tf_op jit(solution)/shard_map/ppermute | solution.py:19
  5.5 1.0 %copy-start = (f32[64,1152]{1,0:T(8,128)S(1)}, f32[64,1152]{1,0:T(8,128)}, u32[]{:S(2)}) copy-start(f32[64,1152]{1,0:T(8,128)} %images.3) | copy-start | bytes 884740
  6.5 21.1 %copy-start.2 = (f32[64,1152]{1,0:T(8,128)S(1)}, f32[64,1152]{1,0:T(8,128)}, u32[]{:S(2)}) copy-start(f32[64,1152]{1,0:T(8,128)} %captions.1) | copy-start | bytes 884740
  6.6 36.0 %collective-permute-start.3 = (f32[72,1152]{1,0:T(8,128)S(1)}, f32[72,1152]{1,0:T(8,128)S(1)}, u32[]{:S(2)}, u32[]{:S(2)}) collective-permute-start(f32[72,1152]{1,0:T(8,128)S(1)} %pack_kernel.1.p0), channel_id=1, source_target_pairs={{0,6},{1,7},{2,0},{3,1},{4,2},{5,3},{6,4},{7,5},{8,14},{9,15},{10,... | collective-permute-start | bytes 995336 | tf_op jit(solution)/shard_map/ppermute | solution.py:24
  11.0 31.6 %collective-permute-start.2 = (f32[72,1152]{1,0:T(8,128)S(1)}, f32[72,1152]{1,0:T(8,128)S(1)}, u32[]{:S(2)}, u32[]{:S(2)}) collective-permute-start(f32[72,1152]{1,0:T(8,128)S(1)} %pack_kernel.1.p0), channel_id=1, source_target_pairs={{0,4},{1,5},{2,6},{3,7},{4,0},{5,1},{6,2},{7,3},{8,12},{9,13},{10,... | collective-permute-start | bytes 995336 | tf_op jit(solution)/shard_map/ppermute | solution.py:24
  13.4 29.2 %collective-permute-start.1 = (f32[72,1152]{1,0:T(8,128)S(1)}, f32[72,1152]{1,0:T(8,128)S(1)}, u32[]{:S(2)}, u32[]{:S(2)}) collective-permute-start(f32[72,1152]{1,0:T(8,128)S(1)} %pack_kernel.1.p0), channel_id=1, source_target_pairs={{0,2},{1,3},{2,4},{3,5},{4,6},{5,7},{6,0},{7,1},{8,10},{9,11},{10,... | collective-permute-start | bytes 995336 | tf_op jit(solution)/shard_map/ppermute | solution.py:24
  25.6 12.7 %collective-permute-start.4 = (f32[64,1152]{1,0:T(8,128)S(1)}, f32[64,1152]{1,0:T(8,128)S(1)}, u32[]{:S(2)}, u32[]{:S(2)}) collective-permute-start(f32[64,1152]{1,0:T(8,128)S(1)} %collective-permute-done.t1), channel_id=1, source_target_pairs={{0,8},{8,16},{16,24},{24,32},{32,40},{40,48},{48,56},{56,64},{64,7... | collective-permute-start | bytes 884744 | tf_op jit(solution)/shard_map/ppermute | solution.py:19
  38.5 6.2 %collective-permute-start.5 = (f32[192,1152]{1,0:T(8,128)S(1)}, f32[192,1152]{1,0:T(8,128)S(1)}, u32[]{:S(2)}, u32[]{:S(2)}) collective-permute-start(f32[192,1152]{1,0:T(8,128)S(1)} %get-tuple-element.32), channel_id=1, source_target_pairs={{0,1},{1,0},{2,3},{3,2},{4,5},{5,4},{6,7},{7,6},{8,9},{9,8},{10,11... | collective-permute-start | bytes 2654216 | tf_op jit(solution)/shard_map/ppermute | solution.py:29
  46.7 4.3 %collective-permute-start.9 = (f32[192,1152]{1,0:T(8,128)S(1)}, f32[192,1152]{1,0:T(8,128)S(1)}, u32[]{:S(2)}, u32[]{:S(2)}) collective-permute-start(f32[192,1152]{1,0:T(8,128)S(1)} %get-tuple-element.45), channel_id=1, source_target_pairs={{0,1},{1,0},{2,3},{3,2},{4,5},{5,4},{6,7},{7,6},{8,9},{9,8},{10,11... | collective-permute-start | bytes 2654216 | tf_op jit(solution)/shard_map/ppermute | solution.py:29
  51.1 13.2 %collective-permute-start.10 = (f32[64,1152]{1,0:T(8,128)S(1)}, f32[64,1152]{1,0:T(8,128)S(1)}, u32[]{:S(2)}, u32[]{:S(2)}) collective-permute-start(f32[64,1152]{1,0:T(8,128)S(1)} %last_kernel.1), channel_id=1, source_target_pairs={{0,760},{8,0},{16,8},{24,16},{32,24},{40,32},{48,40},{56,48},{64,5... | collective-permute-start | bytes 884744 | tf_op jit(solution)/shard_map/ppermute | solution.py:19
  55.0 13.5 %collective-permute-start.6 = (f32[64,1152]{1,0:T(8,128)S(1)}, f32[64,1152]{1,0:T(8,128)S(1)}, u32[]{:S(2)}, u32[]{:S(2)}) collective-permute-start(f32[64,1152]{1,0:T(8,128)S(1)} %get-tuple-element.41), channel_id=1, source_target_pairs={{0,4},{1,5},{2,6},{3,7},{4,0},{5,1},{6,2},{7,3},{8,12},{9,13},{10,... | collective-permute-start | bytes 884744 | tf_op jit(solution)/shard_map/ppermute | solution.py:24
  58.2 13.7 %collective-permute-start.7 = (f32[64,1152]{1,0:T(8,128)S(1)}, f32[64,1152]{1,0:T(8,128)S(1)}, u32[]{:S(2)}, u32[]{:S(2)}) collective-permute-start(f32[64,1152]{1,0:T(8,128)S(1)} %get-tuple-element.42), channel_id=1, source_target_pairs={{0,6},{1,7},{2,0},{3,1},{4,2},{5,3},{6,4},{7,5},{8,14},{9,15},{10,... | collective-permute-start | bytes 884744 | tf_op jit(solution)/shard_map/ppermute | solution.py:24
  62.2 11.5 %copy-start.1 = (f32[64,1152]{1,0:T(8,128)S(1)}, f32[64,1152]{1,0:T(8,128)}, u32[]{:S(2)}) copy-start(f32[64,1152]{1,0:T(8,128)} %images.3) | copy-start | bytes 884740
  62.2 10.7 %collective-permute-start.8 = (f32[64,1152]{1,0:T(8,128)S(1)}, f32[64,1152]{1,0:T(8,128)S(1)}, u32[]{:S(2)}, u32[]{:S(2)}) collective-permute-start(f32[64,1152]{1,0:T(8,128)S(1)} %get-tuple-element.43), channel_id=1, source_target_pairs={{0,2},{1,3},{2,4},{3,5},{4,6},{5,7},{6,0},{7,1},{8,10},{9,11},{10,... | collective-permute-start | bytes 884744 | tf_op jit(solution)/shard_map/ppermute | solution.py:24
  64.4 9.3 %collective-permute-start.11 = (f32[64,1152]{1,0:T(8,128)S(1)}, f32[64,1152]{1,0:T(8,128)S(1)}, u32[]{:S(2)}, u32[]{:S(2)}) collective-permute-start(f32[64,1152]{1,0:T(8,128)S(1)} %middle_kernel.1), channel_id=1, source_target_pairs={{0,760},{8,0},{16,8},{24,16},{32,24},{40,32},{48,40},{56,48},{64,5... | collective-permute-start | bytes 884744 | tf_op jit(solution)/shard_map/ppermute | solution.py:19

commit v2 on v1

--- a/solution.py
+++ b/solution.py
@@ -21,7 +21,8 @@
 
 def along_x(shard, by):
     count = lax.axis_size("group")
-    return lax.ppermute(shard, "group", [(i, (i + 2 * by) % count) for i in range(count)])
+    pairs = [(i, (i + (2 * by if i % 2 == 0 else -2 * by)) % count) for i in range(count)]
+    return lax.ppermute(shard, "group", pairs)
 
 
 def across_cores(shard):
@@ -100,12 +101,12 @@
             t_high[at : at + 32, :], t_low[at : at + 32, :] = split(unit)
 
     def wide(value):
-        return jnp.broadcast_to(value, (1, scalars.shape[1]))
-
-    scalars[0:1, :] = jnp.exp(wide(log_scale[...]))
-    scalars[1:2, :] = wide(logit_bias[...])
+        return jnp.full((1, scalars.shape[1]), value, jnp.float32)
+
+    scalars[0:1, :] = jnp.exp(wide(log_scale[0]))
+    scalars[1:2, :] = wide(logit_bias[0])
     for k in range(2 * WIN):
-        scalars[2 + k : 3 + k, :] = wide(places[0:1, k : k + 1])
+        scalars[2 + k : 3 + k, :] = wide(places[k].astype(jnp.float32))
 
 
 def late_kernel(t2, early_units, early_high, early_low, units, t_high, t_low):
@@ -168,6 +169,10 @@
     out[...] = (own[ROWS : 2 * ROWS, :] + other[ROWS : 2 * ROWS, :]) + back[...]
 
 
+def add_kernel(a, b, out):
+    out[...] = a[...] + b[...]
+
+
 def finish(values, grad, temper):
     inverse = lax.rsqrt(jnp.sum(values * values, axis=-1, keepdims=True) + EPS)
     unit = values * inverse
@@ -177,17 +182,18 @@
 
 
 def final_kernel(
-    scalars, images, captions, i0, i1, i2, i3, own, other, back, out_images, out_captions
+    scalars, images, captions, i0, i1, i3, own, other, back, out_images, out_captions
 ):
     temper = scalars[0:1, 0:1]
     for r in range(0, ROWS, 32):
         at = slice(r, r + 32)
         grad = (own[at, :] + other[at, :]) + back[at, :]
         out_captions[at, :] = finish(captions[at, :], grad, temper)
-        grad = (i0[at, :] + i1[at, :]) + (i2[at, :] + i3[at, :])
+        grad = (i0[at, :] + i1[at, :]) + i3[at, :]
         out_images[at, :] = finish(images[at, :], grad, temper)
 
 
+SMEM = pl.BlockSpec(memory_space=pltpu.SMEM)
 VMEM = pl.BlockSpec(memory_space=pltpu.VMEM)
 HBM = pl.BlockSpec(memory_space=pl.ANY)
 
@@ -200,10 +206,10 @@
     return jax.ShapeDtypeStruct(shape, jnp.bfloat16)
 
 
-def call(kernel, inputs, outs, products):
+def call(kernel, inputs, outs, products, smem=0):
     return pl.pallas_call(
         kernel,
-        in_specs=[VMEM] * inputs,
+        in_specs=[SMEM] * smem + [VMEM] * (inputs - smem),
         out_specs=[VMEM] * len(outs),
         out_shape=outs,
         compiler_params=pltpu.CompilerParams(vmem_limit_bytes=VMEM_LIMIT),
@@ -237,17 +243,19 @@
         compiler_params=pltpu.CompilerParams(vmem_limit_bytes=VMEM_LIMIT),
         name="pack_kernel",
     )(images, labels[None, :])
-    pack2, pack1, pack3 = (along_x(pack, k) for k in (2, 1, 3))
+    pack1 = along_x(pack, 1)
+    pack3 = along_x(pack, -1)
+    pack2 = along_x(pack1, 1)
 
     places = []
     for who in (member, member ^ 1):
         for stride in range(WIN):
             source = (position - stride) % cycle_size
             places.append(source * (members * ROWS) + who * ROWS)
-    places = jnp.stack(places).astype(jnp.float32)[None, :]
+    places = jnp.stack(places)
     scalars, *early = call(
-        early_kernel, 5, [f32(8, 128), f32(2 * ROWS, D)] + [b16(2 * ROWS, D)] * 2, 60
-    )(log_scale[None, :], logit_bias[None, :], places, captions, text1)
+        early_kernel, 5, [f32(8, 128), f32(2 * ROWS, D)] + [b16(2 * ROWS, D)] * 2, 60, 3
+    )(log_scale, logit_bias, places, captions, text1)
     units, t_high, t_low = call(late_kernel, 4, [f32(texts_all, D)] + text_halves, 0)(
         text2, *early
     )
@@ -278,19 +286,21 @@
     back = along_loop(back, -1)
     (back,) = call(middle_kernel, 3, [f32(ROWS, D)], 0)(own_text, other_text, back)
     back = along_loop(back, -1)
-    i2, i1, i3 = along_x(i2, -2), along_x(i1, -1), along_x(i3, -3)
+    (i1,) = call(add_kernel, 2, [f32(ROWS, D)], 0)(i1, along_x(i2, -1))
+    i1 = along_x(i1, -1)
+    i3 = along_x(i3, 1)
 
     first = pl.BlockSpec((ROWS, D), lambda i: (0, 0))
     return tuple(
         pl.pallas_call(
             final_kernel,
             grid=(1,),
-            in_specs=[pl.BlockSpec((8, 128), lambda i: (0, 0))] + [first] * 9,
+            in_specs=[pl.BlockSpec((8, 128), lambda i: (0, 0))] + [first] * 8,
             out_specs=[first] * 2,
             out_shape=[f32(ROWS, D)] * 2,
             compiler_params=pltpu.CompilerParams(vmem_limit_bytes=VMEM_LIMIT),
             name="finish",
-        )(scalars, images, captions, i0, i2, i1, i3, own_text, other_text, back)
+        )(scalars, images, captions, i0, i1, i3, own_text, other_text, back)
     )
 
 

time: 75.9 us -> 81.9 us (1.079)
  waiting for transfers between devices: 24.9 us -> 32 us
  starting transfers between devices: 39.5 us -> 37.9 us
    ppermute x4, waiting for transfers between devices: 19.6 us -> 32 us  [along_loop(): lax.ppermute(shard, 'loop', [(i, (i + by) % count) for i in range(count)])]
    ppermute x6, waiting for transfers between devices: 4.44 us -> 0.02 us  [along_x(): return lax.ppermute(shard, 'group', pairs)]
    ppermute x6, starting transfers between devices: 18.6 us -> 17.7 us  [along_x(): return lax.ppermute(shard, 'group', pairs)]
    ppermute x2, waiting for transfers between devices: 0.94 us -> 0.01 us  [across_cores(): return lax.ppermute(shard, 'group', [(i, i ^ 1) for i in range(count)])]
    ppermute x2, starting transfers between devices: 6.2 us -> 5.28 us  [across_cores(): return lax.ppermute(shard, 'group', [(i, i ^ 1) for i in range(count)])]
  transfers between devices with their start and end apart: 12 -> 12, of which waited for: 6 -> 4; matrix products, arithmetic and copies ran while one was open for 0% -> 0% of each run, Pallas kernels for 5% -> 5%
where the time goes in v2:
time: 81.9 us; the launch traced here: 81.4 us
  starting transfers between devices  37.9 us (46%)
  waiting for transfers between devices  32 us (39%)
  Pallas kernels  7.59 us (9%)
  between operations  2.22 us (3%)
  local copies, waits for them, and re-layouts  1.7 us (2%)
    ppermute x4, waiting for transfers between devices, along_loop(): lax.ppermute(shard, 'loop', [(i, (i + by) % count) for i in range(count)])  32 us
    ppermute x6, starting transfers between devices, along_x(): return lax.ppermute(shard, 'group', pairs)  17.7 us
    ppermute x4, starting transfers between devices, along_loop(): lax.ppermute(shard, 'loop', [(i, (i + by) % count) for i in range(count)])  15 us
    ppermute x2, starting transfers between devices, across_cores(): return lax.ppermute(shard, 'group', [(i, i ^ 1) for i in range(count)])  5.28 us
    pallas_call x1, Pallas kernels, per_device(): call(own_kernel, 7, image_halves + [f32(8, images_all)] + weight_halves +...  2.13 us
    pallas_call x1, Pallas kernels, per_device(): call(cross_kernel, 5, text_halves + weight_halves + [f32(texts_all, D)], 2)  1.96 us
  transfers between devices with their start and end apart: 12, of which 4 were waited for; matrix products, arithmetic and copies ran while one was open for 0% of the time, Pallas kernels for 5%

profile of v2, /device:TPU:1, one launch (start us, length us, event | category | flops | bytes accessed | tf_op | source)
XLA Modules:
  0.0 81.4 jit_solution(2038250891893933601)
XLA Ops:
  0.6 0.0 copy-start.3
  0.6 0.6 copy-done.3
  1.3 0.0 copy-start
  1.3 1.0 %copy-done = f32[64,1152]{1,0:T(8,128)S(1)} copy-done((f32[64,1152]{1,0:T(8,128)S(1)}, f32[64,1152]{1,0:T(8,128)}, u32[]{:S(2)}) %copy-start) | copy-done | bytes 294936
  2.2 0.0 copy-start.2
  2.3 0.2 pack_kernel.1.p0
  2.4 5.2 %collective-permute-start.1 = (f32[72,1152]{1,0:T(8,128)S(1)}, f32[72,1152]{1,0:T(8,128)S(1)}, u32[]{:S(2)}, u32[]{:S(2)}) collective-permute-start(f32[72,1152]{1,0:T(8,128)S(1)} %pack_kernel.1.p0), channel_id=1, source_target_pairs={{0,2},{1,7},{2,4},{3,1},{4,6},{5,3},{6,0},{7,5},{8,10},{9,15},{10,... | collective-permute-start | bytes 995336 | tf_op jit(solution)/shard_map/ppermute | solution.py:25
  7.6 0.0 copy-done.2
  7.6 4.0 %collective-permute-start = (f32[64,1152]{1,0:T(8,128)S(1)}, f32[64,1152]{1,0:T(8,128)S(1)}, u32[]{:S(2)}, u32[]{:S(2)}) collective-permute-start(f32[64,1152]{1,0:T(8,128)S(1)} %copy-done.2), channel_id=1, source_target_pairs={{0,8},{8,16},{16,24},{24,32},{32,40},{40,48},{48,56},{56,64},{64,7... | collective-permute-start | bytes 884744 | tf_op jit(solution)/shard_map/ppermute | solution.py:19
  11.7 1.9 %collective-permute-start.3 = (f32[72,1152]{1,0:T(8,128)S(1)}, f32[72,1152]{1,0:T(8,128)S(1)}, u32[]{:S(2)}, u32[]{:S(2)}) collective-permute-start(f32[72,1152]{1,0:T(8,128)S(1)} %pack_kernel.1.p0), channel_id=1, source_target_pairs={{0,6},{1,3},{2,0},{3,5},{4,2},{5,7},{6,4},{7,1},{8,14},{9,11},{10,... | collective-permute-start | bytes 995336 | tf_op jit(solution)/shard_map/ppermute | solution.py:25
  14.9 0.1 stack.27.places
  15.0 17.1 %collective-permute-done.t1 = f32[64,1152]{1,0:T(8,128)S(1)} collective-permute-done((f32[64,1152]{1,0:T(8,128)S(1)}, f32[64,1152]{1,0:T(8,128)S(1)}, u32[]{:S(2)}, u32[]{:S(2)}) %collective-permute-start) | collective-permute-done | bytes 294944 | tf_op jit(solution)/shard_map/ppermute | solution.py:19
  32.1 1.9 %collective-permute-start.4 = (f32[64,1152]{1,0:T(8,128)S(1)}, f32[64,1152]{1,0:T(8,128)S(1)}, u32[]{:S(2)}, u32[]{:S(2)}) collective-permute-start(f32[64,1152]{1,0:T(8,128)S(1)} %collective-permute-done.t1), channel_id=1, source_target_pairs={{0,8},{8,16},{16,24},{24,32},{32,40},{40,48},{48,56},{56,64},{64,7... | collective-permute-start | bytes 884744 | tf_op jit(solution)/shard_map/ppermute | solution.py:19
  34.1 0.0 collective-permute-done.1.p1
  34.1 2.0 %collective-permute-start.2 = (f32[72,1152]{1,0:T(8,128)S(1)}, f32[72,1152]{1,0:T(8,128)S(1)}, u32[]{:S(2)}, u32[]{:S(2)}) collective-permute-start(f32[72,1152]{1,0:T(8,128)S(1)} %collective-permute-done.1.p1), channel_id=1, source_target_pairs={{0,2},{1,7},{2,4},{3,1},{4,6},{5,3},{6,0},{7,5},{8,10},{9,15},{10,... | collective-permute-start | bytes 995336 | tf_op jit(solution)/shard_map/ppermute | solution.py:25
  36.1 0.7 early_kernel.1
  36.8 8.7 %collective-permute-done.4.t2 = f32[64,1152]{1,0:T(8,128)S(1)} collective-permute-done((f32[64,1152]{1,0:T(8,128)S(1)}, f32[64,1152]{1,0:T(8,128)S(1)}, u32[]{:S(2)}, u32[]{:S(2)}) %collective-permute-start.4) | collective-permute-done | bytes 294944 | tf_op jit(solution)/shard_map/ppermute | solution.py:19
  45.5 0.2 late_kernel.1
  45.7 3.1 %collective-permute-start.5 = (f32[192,1152]{1,0:T(8,128)S(1)}, f32[192,1152]{1,0:T(8,128)S(1)}, u32[]{:S(2)}, u32[]{:S(2)}) collective-permute-start(f32[192,1152]{1,0:T(8,128)S(1)} %get-tuple-element.32), channel_id=1, source_target_pairs={{0,1},{1,0},{2,3},{3,2},{4,5},{5,4},{6,7},{7,6},{8,9},{9,8},{10,11... | collective-permute-start | bytes 2654216 | tf_op jit(solution)/shard_map/ppermute | solution.py:30
  48.9 0.0 collective-permute-done.3.p3
  48.9 0.0 collective-permute-done.2.p2
  48.9 2.1 %own_kernel.1 = (bf16[256,1152]{1,0:T(8,128)(2,1)S(1)}, bf16[256,1152]{1,0:T(8,128)(2,1)S(1)}, f32[8,256]{1,0:T(8,128)S(1)}, bf16[192,256]{1,0:T(8,128)(2,1)S(1)...) custom-call(f32[8,128]{1,0:T(8,128)S(1)} %get-tuple-element.24.scalars, f32[72,1152]{1,0:T(8,128)S(1)} %pack_kernel.1.p0, ...), custom_call_target="tpu_custom_call" | custom-call | flops 20384317440 | bytes 7077888 | tf_op jit(solution)/shard_map/own_kernel/pallas_call | solution.py:265
  51.0 0.0 collective-permute-done.5.units
  51.0 2.0 %cross_kernel.1 = (bf16[192,1152]{1,0:T(8,128)(2,1)S(1)}, bf16[192,1152]{1,0:T(8,128)(2,1)S(1)}, bf16[192,256]{1,0:T(8,128)(2,1)S(1)}, bf16[192,256]{1,0:T(8,128)(2,1)S(1)}, f32[192,1152]{1,0:T(8,128)S(1)}) custom-call(f32[8,128]{1,0:T(8,128)S(1)} %get-tuple-element.24.scalars, f32[192,1152]{1,0:T(8,128)S(1)} %collective-permute-done.5.units, ...), custom_call_target="tpu_custom_call" | custom-call | flops 679477248 | bytes 7077888 | tf_op jit(solution)/shard_map/cross_kernel/pallas_call | solution.py:271
  53.0 2.1 %collective-permute-start.9 = (f32[192,1152]{1,0:T(8,128)S(1)}, f32[192,1152]{1,0:T(8,128)S(1)}, u32[]{:S(2)}, u32[]{:S(2)}) collective-permute-start(f32[192,1152]{1,0:T(8,128)S(1)} %get-tuple-element.45), channel_id=1, source_target_pairs={{0,1},{1,0},{2,3},{3,2},{4,5},{5,4},{6,7},{7,6},{8,9},{9,8},{10,11... | collective-permute-start | bytes 2654216 | tf_op jit(solution)/shard_map/ppermute | solution.py:30
  55.1 1.2 %image_kernel.1 = (f32[64,1152]{1,0:T(8,128)S(1)}, f32[64,1152]{1,0:T(8,128)S(1)}, f32[64,1152]{1,0:T(8,128)S(1)}, f32[64,1152]{1,0:T(8,128)S(1)}) custom-call(bf16[192,256]{1,0:T(8,128)(2,1)S(1)} %get-tuple-element.30.w_high, bf16[192,256]{1,0:T(8,128)(2,1)S(1)} %get-tuple-element.31.w_low, bf16[192,1152]{1,0:T(8,128)(2,1)S(1)} %get-tuple-element.28.t_high, ...), custom_call_target="tpu_custom_call" | custom-call | flops 679477248 | bytes 7077888 | tf_op jit(solution)/shard_map/image_kernel/pallas_call | solution.py:275
  56.4 1.9 %collective-permute-start.6 = (f32[64,1152]{1,0:T(8,128)S(1)}, f32[64,1152]{1,0:T(8,128)S(1)}, u32[]{:S(2)}, u32[]{:S(2)}) collective-permute-start(f32[64,1152]{1,0:T(8,128)S(1)} %get-tuple-element.42), channel_id=1, source_target_pairs={{0,6},{1,3},{2,0},{3,5},{4,2},{5,7},{6,4},{7,1},{8,14},{9,11},{10,... | collective-permute-start | bytes 884744 | tf_op jit(solution)/shard_map/ppermute | solution.py:25
  58.3 0.0 collective-permute-done.9.other
  58.4 2.5 %collective-permute-start.10 = (f32[64,1152]{1,0:T(8,128)S(1)}, f32[64,1152]{1,0:T(8,128)S(1)}, u32[]{:S(2)}, u32[]{:S(2)}) collective-permute-start(f32[64,1152]{1,0:T(8,128)S(1)} %last_kernel.1), channel_id=1, source_target_pairs={{0,760},{8,0},{16,8},{24,16},{32,24},{40,32},{48,40},{56,48},{64,5... | collective-permute-start | bytes 884744 | tf_op jit(solution)/shard_map/ppermute | solution.py:19
  60.9 4.6 %collective-permute-start.8 = (f32[64,1152]{1,0:T(8,128)S(1)}, f32[64,1152]{1,0:T(8,128)S(1)}, u32[]{:S(2)}, u32[]{:S(2)}) collective-permute-start(f32[64,1152]{1,0:T(8,128)S(1)} %get-tuple-element.43), channel_id=1, source_target_pairs={{0,2},{1,7},{2,4},{3,1},{4,6},{5,3},{6,0},{7,5},{8,10},{9,15},{10,... | collective-permute-start | bytes 884744 | tf_op jit(solution)/shard_map/ppermute | solution.py:25
  65.5 0.0 collective-permute-done.6.b
  65.5 0.0 copy-start.1
  65.6 2.1 %collective-permute-start.7 = (f32[64,1152]{1,0:T(8,128)S(1)}, f32[64,1152]{1,0:T(8,128)S(1)}, u32[]{:S(2)}, u32[]{:S(2)}) collective-permute-start(f32[64,1152]{1,0:T(8,128)S(1)} %add_kernel.1), channel_id=1, source_target_pairs={{0,6},{1,3},{2,0},{3,5},{4,2},{5,7},{6,4},{7,1},{8,14},{9,11},{10,... | collective-permute-start | bytes 884744 | tf_op jit(solution)/shard_map/ppermute | solution.py:25
  67.6 0.6 collective-permute-done.10.back
  68.2 0.1 middle_kernel.1
  68.3 6.5 %collective-permute-start.11 = (f32[64,1152]{1,0:T(8,128)S(1)}, f32[64,1152]{1,0:T(8,128)S(1)}, u32[]{:S(2)}, u32[]{:S(2)}) collective-permute-start(f32[64,1152]{1,0:T(8,128)S(1)} %middle_kernel.1), channel_id=1, source_target_pairs={{0,760},{8,0},{16,8},{24,16},{32,24},{40,32},{48,40},{56,48},{64,5... | collective-permute-start | bytes 884744 | tf_op jit(solution)/shard_map/ppermute | solution.py:19
  74.8 0.0 collective-permute-done.8.i3
  74.8 0.0 collective-permute-done.7.i1
  74.8 5.5 %collective-permute-done.11.back = f32[64,1152]{1,0:T(8,128)S(1)} collective-permute-done((f32[64,1152]{1,0:T(8,128)S(1)}, f32[64,1152]{1,0:T(8,128)S(1)}, u32[]{:S(2)}, u32[]{:S(2)}) %collective-permute-start.11) | collective-permute-done | bytes 294944 | tf_op jit(solution)/shard_map/ppermute | solution.py:19
  80.3 0.0 copy-done.1
  80.3 1.1 %finish.1 = (f32[64,1152]{1,0:T(8,128)}, f32[64,1152]{1,0:T(8,128)}) custom-call(f32[8,128]{1,0:T(8,128)S(1)} %get-tuple-element.24.scalars, f32[64,1152]{1,0:T(8,128)S(1)} %copy-done.1, f32[64,1152]{1,0:T(8,128)S(1)} %copy-done.2, f32[64,1152]{1,0:T(8,128)S(1)} %get-tuple-element.40.after.i0, f32[64,1152]{1,0:T(8,128)S(1)} %collective-permute-done.7.i1, ...), custom_call_target="tpu_custom_call" | custom-call | tf_op jit(solution)/shard_map/finish/pallas_call | solution.py:295
  (2 shorter events, 0.1 us)
Async XLA Ops:
  0.6 0.7 copy-start.3
  1.3 1.0 %copy-start = (f32[64,1152]{1,0:T(8,128)S(1)}, f32[64,1152]{1,0:T(8,128)}, u32[]{:S(2)}) copy-start(f32[64,1152]{1,0:T(8,128)} %images.3) | copy-start | bytes 884740
  2.2 5.4 %copy-start.2 = (f32[64,1152]{1,0:T(8,128)S(1)}, f32[64,1152]{1,0:T(8,128)}, u32[]{:S(2)}) copy-start(f32[64,1152]{1,0:T(8,128)} %captions.1) | copy-start | bytes 884740
  2.4 31.7 %collective-permute-start.1 = (f32[72,1152]{1,0:T(8,128)S(1)}, f32[72,1152]{1,0:T(8,128)S(1)}, u32[]{:S(2)}, u32[]{:S(2)}) collective-permute-start(f32[72,1152]{1,0:T(8,128)S(1)} %pack_kernel.1.p0), channel_id=1, source_target_pairs={{0,2},{1,7},{2,4},{3,1},{4,6},{5,3},{6,0},{7,5},{8,10},{9,15},{10,... | collective-permute-start | bytes 995336 | tf_op jit(solution)/shard_map/ppermute | solution.py:25
  7.6 24.5 %collective-permute-start = (f32[64,1152]{1,0:T(8,128)S(1)}, f32[64,1152]{1,0:T(8,128)S(1)}, u32[]{:S(2)}, u32[]{:S(2)}) collective-permute-start(f32[64,1152]{1,0:T(8,128)S(1)} %copy-done.2), channel_id=1, source_target_pairs={{0,8},{8,16},{16,24},{24,32},{32,40},{40,48},{48,56},{56,64},{64,7... | collective-permute-start | bytes 884744 | tf_op jit(solution)/shard_map/ppermute | solution.py:19
  11.7 37.2 %collective-permute-start.3 = (f32[72,1152]{1,0:T(8,128)S(1)}, f32[72,1152]{1,0:T(8,128)S(1)}, u32[]{:S(2)}, u32[]{:S(2)}) collective-permute-start(f32[72,1152]{1,0:T(8,128)S(1)} %pack_kernel.1.p0), channel_id=1, source_target_pairs={{0,6},{1,3},{2,0},{3,5},{4,2},{5,7},{6,4},{7,1},{8,14},{9,11},{10,... | collective-permute-start | bytes 995336 | tf_op jit(solution)/shard_map/ppermute | solution.py:25
  32.1 13.4 %collective-permute-start.4 = (f32[64,1152]{1,0:T(8,128)S(1)}, f32[64,1152]{1,0:T(8,128)S(1)}, u32[]{:S(2)}, u32[]{:S(2)}) collective-permute-start(f32[64,1152]{1,0:T(8,128)S(1)} %collective-permute-done.t1), channel_id=1, source_target_pairs={{0,8},{8,16},{16,24},{24,32},{32,40},{40,48},{48,56},{56,64},{64,7... | collective-permute-start | bytes 884744 | tf_op jit(solution)/shard_map/ppermute | solution.py:19
  34.1 14.8 %collective-permute-start.2 = (f32[72,1152]{1,0:T(8,128)S(1)}, f32[72,1152]{1,0:T(8,128)S(1)}, u32[]{:S(2)}, u32[]{:S(2)}) collective-permute-start(f32[72,1152]{1,0:T(8,128)S(1)} %collective-permute-done.1.p1), channel_id=1, source_target_pairs={{0,2},{1,7},{2,4},{3,1},{4,6},{5,3},{6,0},{7,5},{8,10},{9,15},{10,... | collective-permute-start | bytes 995336 | tf_op jit(solution)/shard_map/ppermute | solution.py:25
  45.7 5.3 %collective-permute-start.5 = (f32[192,1152]{1,0:T(8,128)S(1)}, f32[192,1152]{1,0:T(8,128)S(1)}, u32[]{:S(2)}, u32[]{:S(2)}) collective-permute-start(f32[192,1152]{1,0:T(8,128)S(1)} %get-tuple-element.32), channel_id=1, source_target_pairs={{0,1},{1,0},{2,3},{3,2},{4,5},{5,4},{6,7},{7,6},{8,9},{9,8},{10,11... | collective-permute-start | bytes 2654216 | tf_op jit(solution)/shard_map/ppermute | solution.py:30
  53.0 5.3 %collective-permute-start.9 = (f32[192,1152]{1,0:T(8,128)S(1)}, f32[192,1152]{1,0:T(8,128)S(1)}, u32[]{:S(2)}, u32[]{:S(2)}) collective-permute-start(f32[192,1152]{1,0:T(8,128)S(1)} %get-tuple-element.45), channel_id=1, source_target_pairs={{0,1},{1,0},{2,3},{3,2},{4,5},{5,4},{6,7},{7,6},{8,9},{9,8},{10,11... | collective-permute-start | bytes 2654216 | tf_op jit(solution)/shard_map/ppermute | solution.py:30
  56.4 9.1 %collective-permute-start.6 = (f32[64,1152]{1,0:T(8,128)S(1)}, f32[64,1152]{1,0:T(8,128)S(1)}, u32[]{:S(2)}, u32[]{:S(2)}) collective-permute-start(f32[64,1152]{1,0:T(8,128)S(1)} %get-tuple-element.42), channel_id=1, source_target_pairs={{0,6},{1,3},{2,0},{3,5},{4,2},{5,7},{6,4},{7,1},{8,14},{9,11},{10,... | collective-permute-start | bytes 884744 | tf_op jit(solution)/shard_map/ppermute | solution.py:25
  58.4 9.9 %collective-permute-start.10 = (f32[64,1152]{1,0:T(8,128)S(1)}, f32[64,1152]{1,0:T(8,128)S(1)}, u32[]{:S(2)}, u32[]{:S(2)}) collective-permute-start(f32[64,1152]{1,0:T(8,128)S(1)} %last_kernel.1), channel_id=1, source_target_pairs={{0,760},{8,0},{16,8},{24,16},{32,24},{40,32},{48,40},{56,48},{64,5... | collective-permute-start | bytes 884744 | tf_op jit(solution)/shard_map/ppermute | solution.py:19
  60.9 13.9 %collective-permute-start.8 = (f32[64,1152]{1,0:T(8,128)S(1)}, f32[64,1152]{1,0:T(8,128)S(1)}, u32[]{:S(2)}, u32[]{:S(2)}) collective-permute-start(f32[64,1152]{1,0:T(8,128)S(1)} %get-tuple-element.43), channel_id=1, source_target_pairs={{0,2},{1,7},{2,4},{3,1},{4,6},{5,3},{6,0},{7,5},{8,10},{9,15},{10,... | collective-permute-start | bytes 884744 | tf_op jit(solution)/shard_map/ppermute | solution.py:25
  65.5 14.8 %copy-start.1 = (f32[64,1152]{1,0:T(8,128)S(1)}, f32[64,1152]{1,0:T(8,128)}, u32[]{:S(2)}) copy-start(f32[64,1152]{1,0:T(8,128)} %images.3) | copy-start | bytes 884740
  65.6 9.3 %collective-permute-start.7 = (f32[64,1152]{1,0:T(8,128)S(1)}, f32[64,1152]{1,0:T(8,128)S(1)}, u32[]{:S(2)}, u32[]{:S(2)}) collective-permute-start(f32[64,1152]{1,0:T(8,128)S(1)} %add_kernel.1), channel_id=1, source_target_pairs={{0,6},{1,3},{2,0},{3,5},{4,2},{5,7},{6,4},{7,1},{8,14},{9,11},{10,... | collective-permute-start | bytes 884744 | tf_op jit(solution)/shard_map/ppermute | solution.py:25
  68.3 12.1 %collective-permute-start.11 = (f32[64,1152]{1,0:T(8,128)S(1)}, f32[64,1152]{1,0:T(8,128)S(1)}, u32[]{:S(2)}, u32[]{:S(2)}) collective-permute-start(f32[64,1152]{1,0:T(8,128)S(1)} %middle_kernel.1), channel_id=1, source_target_pairs={{0,760},{8,0},{16,8},{24,16},{32,24},{40,32},{48,40},{56,48},{64,5... | collective-permute-start | bytes 884744 | tf_op jit(solution)/shard_map/ppermute | solution.py:19

commit v3 on v2

--- a/solution.py
+++ b/solution.py
@@ -92,33 +92,43 @@
     images_in.wait()
 
 
-def early_kernel(log_scale, logit_bias, places, t0, t1, scalars, units, t_high, t_low):
-    for k, text in enumerate((t0, t1)):
-        for r in range(0, ROWS, 32):
-            at = k * ROWS + r
-            unit = unit_rows(text[r : r + 32, :])
-            units[at : at + 32, :] = unit
-            t_high[at : at + 32, :], t_low[at : at + 32, :] = split(unit)
+def unit_kernel(text, unit):
+    for r in range(0, ROWS, 32):
+        unit[r : r + 32, :] = unit_rows(text[r : r + 32, :])
+
+
+def early_kernel(
+    log_scale, logit_bias, places, t0, u1, scalars, units, t_high, t_low, numbers, sem
+):
+    copies = [
+        pltpu.make_async_copy(log_scale, numbers.at[0], sem.at[0]),
+        pltpu.make_async_copy(logit_bias, numbers.at[1], sem.at[1]),
+    ]
+    for copy in copies:
+        copy.start()
+    for r in range(0, 2 * ROWS, 32):
+        unit = unit_rows(t0[r : r + 32, :]) if r < ROWS else u1[r - ROWS : r - ROWS + 32, :]
+        units[r : r + 32, :] = unit
+        t_high[r : r + 32, :], t_low[r : r + 32, :] = split(unit)
+    for copy in copies:
+        copy.wait()
 
     def wide(value):
         return jnp.full((1, scalars.shape[1]), value, jnp.float32)
 
-    scalars[0:1, :] = jnp.exp(wide(log_scale[0]))
-    scalars[1:2, :] = wide(logit_bias[0])
+    scalars[0:1, :] = jnp.exp(wide(numbers[0, 0]))
+    scalars[1:2, :] = wide(numbers[1, 0])
     for k in range(2 * WIN):
         scalars[2 + k : 3 + k, :] = wide(places[k].astype(jnp.float32))
 
 
-def late_kernel(t2, early_units, early_high, early_low, units, t_high, t_low):
+def late_kernel(u2, early_units, early_high, early_low, units, t_high, t_low):
     early = 2 * ROWS
     units[:early, :] = early_units[...]
     t_high[:early, :] = early_high[...]
     t_low[:early, :] = early_low[...]
-    for r in range(0, ROWS, 32):
-        at = early + r
-        unit = unit_rows(t2[r : r + 32, :])
-        units[at : at + 32, :] = unit
-        t_high[at : at + 32, :], t_low[at : at + 32, :] = split(unit)
+    units[early:, :] = u2[...]
+    t_high[early:, :], t_low[early:, :] = split(u2[...])
 
 
 def own_kernel(
@@ -160,17 +170,15 @@
         out[...] = total[k * ROWS : (k + 1) * ROWS, :]
 
 
-def last_kernel(own, other, after, out):
+def last_kernel(own, other, image_part, out, passed):
     at = (WIN - 1) * ROWS
     out[...] = own[at:, :] + other[at:, :]
-
-
-def middle_kernel(own, other, back, out):
-    out[...] = (own[ROWS : 2 * ROWS, :] + other[ROWS : 2 * ROWS, :]) + back[...]
-
-
-def add_kernel(a, b, out):
-    out[...] = a[...] + b[...]
+    passed[...] = image_part[...]
+
+
+def middle_kernel(back, moved, own, other, part, out_text, out_image):
+    out_text[...] = (own[ROWS : 2 * ROWS, :] + other[ROWS : 2 * ROWS, :]) + back[...]
+    out_image[...] = part[...] + moved[...]
 
 
 def finish(values, grad, temper):
@@ -233,7 +241,16 @@
     text_halves = [b16(texts_all, D)] * 2
 
     text1 = along_loop(captions, 1)
-    text2 = along_loop(text1, 1)
+    unit1 = pl.pallas_call(
+        unit_kernel,
+        in_specs=[VMEM],
+        out_specs=VMEM,
+        out_shape=f32(ROWS, D),
+        compiler_params=pltpu.CompilerParams(vmem_limit_bytes=VMEM_LIMIT),
+        cost_estimate=pl.CostEstimate(flops=2000000000, bytes_accessed=ROWS * D * 8, transcendentals=ROWS),
+        name="unit_kernel",
+    )(text1)
+    unit2 = along_loop(unit1, 1)
     pack = pl.pallas_call(
         pack_kernel,
         in_specs=[HBM, HBM],
@@ -253,11 +270,20 @@
             source = (position - stride) % cycle_size
             places.append(source * (members * ROWS) + who * ROWS)
     places = jnp.stack(places)
-    scalars, *early = call(
-        early_kernel, 5, [f32(8, 128), f32(2 * ROWS, D)] + [b16(2 * ROWS, D)] * 2, 60, 3
-    )(log_scale, logit_bias, places, captions, text1)
+    scalars, *early = pl.pallas_call(
+        early_kernel,
+        in_specs=[HBM, HBM, SMEM, VMEM, VMEM],
+        out_specs=[VMEM] * 4,
+        out_shape=[f32(8, 128), f32(2 * ROWS, D)] + [b16(2 * ROWS, D)] * 2,
+        scratch_shapes=[pltpu.SMEM((2, 1), jnp.float32), pltpu.SemaphoreType.DMA((2,))],
+        compiler_params=pltpu.CompilerParams(vmem_limit_bytes=VMEM_LIMIT),
+        cost_estimate=pl.CostEstimate(
+            flops=60 * 6 * X * ROWS * WIN * ROWS * D, bytes_accessed=6 * X * ROWS * D * 4, transcendentals=0
+        ),
+        name="early_kernel",
+    )(log_scale, logit_bias, places, captions, unit1)
     units, t_high, t_low = call(late_kernel, 4, [f32(texts_all, D)] + text_halves, 0)(
-        text2, *early
+        unit2, *early
     )
     other_units = across_cores(units)
 
@@ -275,19 +301,21 @@
     i0, i1, i2, i3 = call(image_kernel, 8, [f32(ROWS, D)] * X, 2)(
         w_high, w_low, t_high, t_low, ow_high, ow_low, ot_high, ot_low
     )
-    back = pl.pallas_call(
+    back, i2 = pl.pallas_call(
         last_kernel,
-        in_specs=[VMEM, VMEM, HBM],
-        out_specs=VMEM,
-        out_shape=f32(ROWS, D),
+        in_specs=[VMEM] * 3,
+        out_specs=[VMEM] * 2,
+        out_shape=[f32(ROWS, D)] * 2,
         compiler_params=pltpu.CompilerParams(vmem_limit_bytes=VMEM_LIMIT),
         name="last_kernel",
-    )(own_text, other_text, i0)
+    )(own_text, other_text, i2)
     back = along_loop(back, -1)
-    (back,) = call(middle_kernel, 3, [f32(ROWS, D)], 0)(own_text, other_text, back)
+    moved = along_x(i2, -1)
+    back, i1 = call(middle_kernel, 5, [f32(ROWS, D)] * 2, 0)(
+        back, moved, own_text, other_text, i1
+    )
+    i1 = along_x(i1, -1)
     back = along_loop(back, -1)
-    (i1,) = call(add_kernel, 2, [f32(ROWS, D)], 0)(i1, along_x(i2, -1))
-    i1 = along_x(i1, -1)
     i3 = along_x(i3, 1)
 
     first = pl.BlockSpec((ROWS, D), lambda i: (0, 0))

time: 81.9 us -> 78 us (0.952)
  the two profiles are of different devices: /device:TPU:1 before, /device:TPU:64 now
where the time goes in v3:
time: 78 us; the launch traced here: 77.6 us
  starting transfers between devices  41.4 us (53%)
  waiting for transfers between devices  24.8 us (32%)
  Pallas kernels  8.09 us (10%)
  between operations  2.19 us (3%)
  local copies, waits for them, and re-layouts  1.05 us (1%)
    ppermute x6, starting transfers between devices, along_x(): return lax.ppermute(shard, 'group', pairs)  21.4 us
    ppermute x4, waiting for transfers between devices, along_loop(): lax.ppermute(shard, 'loop', [(i, (i + by) % count) for i in range(count)])  17.2 us
    ppermute x4, starting transfers between devices, along_loop(): lax.ppermute(shard, 'loop', [(i, (i + by) % count) for i in range(count)])  15.9 us
    ppermute x6, waiting for transfers between devices, along_x(): return lax.ppermute(shard, 'group', pairs)  6.5 us
    ppermute x2, starting transfers between devices, across_cores(): return lax.ppermute(shard, 'group', [(i, i ^ 1) for i in range(count)])  4.1 us
    pallas_call x1, Pallas kernels, per_device(): call(own_kernel, 7, image_halves + [f32(8, images_all)] + weight_halves +...  2.13 us
    pallas_call x1, Pallas kernels, per_device(): call(cross_kernel, 5, text_halves + weight_halves + [f32(texts_all, D)], 2)  1.96 us
  transfers between devices with their start and end apart: 12, of which 8 were waited for; matrix products, arithmetic and copies ran while one was open for 0% of the time, Pallas kernels for 6%

profile of v3, /device:TPU:64, one launch (start us, length us, event | category | flops | bytes accessed | tf_op | source)
XLA Modules:
  0.0 77.6 jit_solution(463742362993491908)
XLA Ops:
  0.6 0.0 copy-start.3
  0.6 4.3 %collective-permute-start = (f32[64,1152]{1,0:T(8,128)}, f32[64,1152]{1,0:T(8,128)S(1)}, u32[]{:S(2)}, u32[]{:S(2)}) collective-permute-start(f32[64,1152]{1,0:T(8,128)} %captions.1), channel_id=1, source_target_pairs={{0,8},{8,16},{16,24},{24,32},{32,40},{40,48},{48,56},{56,64},{64,7... | collective-permute-start | bytes 884744 | tf_op jit(solution)/shard_map/ppermute | solution.py:19
  4.9 0.0 copy-done.3
  4.9 0.0 copy-start
  5.0 1.0 %copy-done = f32[64,1152]{1,0:T(8,128)S(1)} copy-done((f32[64,1152]{1,0:T(8,128)S(1)}, f32[64,1152]{1,0:T(8,128)}, u32[]{:S(2)}) %copy-start) | copy-done | bytes 294936
  5.9 0.2 pack_kernel.1.p0
  6.1 3.4 %collective-permute-start.1 = (f32[72,1152]{1,0:T(8,128)S(1)}, f32[72,1152]{1,0:T(8,128)S(1)}, u32[]{:S(2)}, u32[]{:S(2)}) collective-permute-start(f32[72,1152]{1,0:T(8,128)S(1)} %pack_kernel.1.p0), channel_id=1, source_target_pairs={{0,2},{1,7},{2,4},{3,1},{4,6},{5,3},{6,0},{7,5},{8,10},{9,15},{10,... | collective-permute-start | bytes 995336 | tf_op jit(solution)/shard_map/ppermute | solution.py:25
  9.5 3.7 %collective-permute-start.3 = (f32[72,1152]{1,0:T(8,128)S(1)}, f32[72,1152]{1,0:T(8,128)S(1)}, u32[]{:S(2)}, u32[]{:S(2)}) collective-permute-start(f32[72,1152]{1,0:T(8,128)S(1)} %pack_kernel.1.p0), channel_id=1, source_target_pairs={{0,6},{1,3},{2,0},{3,5},{4,2},{5,7},{6,4},{7,1},{8,14},{9,11},{10,... | collective-permute-start | bytes 995336 | tf_op jit(solution)/shard_map/ppermute | solution.py:25
  14.5 0.1 stack.27.places
  14.6 0.0 copy-start.2
  14.6 1.5 %collective-permute-done.text = f32[64,1152]{1,0:T(8,128)S(1)} collective-permute-done((f32[64,1152]{1,0:T(8,128)}, f32[64,1152]{1,0:T(8,128)S(1)}, u32[]{:S(2)}, u32[]{:S(2)}) %collective-permute-start) | collective-permute-done | bytes 294944 | tf_op jit(solution)/shard_map/ppermute | solution.py:19
  16.1 0.1 unit_kernel.1.u1
  16.2 2.7 %collective-permute-start.4 = (f32[64,1152]{1,0:T(8,128)S(1)}, f32[64,1152]{1,0:T(8,128)S(1)}, u32[]{:S(2)}, u32[]{:S(2)}) collective-permute-start(f32[64,1152]{1,0:T(8,128)S(1)} %unit_kernel.1.u1), channel_id=1, source_target_pairs={{0,8},{8,16},{16,24},{24,32},{32,40},{40,48},{48,56},{56,64},{64,7... | collective-permute-start | bytes 884744 | tf_op jit(solution)/shard_map/ppermute | solution.py:19
  19.0 0.0 collective-permute-done.1.p1
  19.0 2.2 %collective-permute-start.2 = (f32[72,1152]{1,0:T(8,128)S(1)}, f32[72,1152]{1,0:T(8,128)S(1)}, u32[]{:S(2)}, u32[]{:S(2)}) collective-permute-start(f32[72,1152]{1,0:T(8,128)S(1)} %collective-permute-done.1.p1), channel_id=1, source_target_pairs={{0,2},{1,7},{2,4},{3,1},{4,6},{5,3},{6,0},{7,5},{8,10},{9,15},{10,... | collective-permute-start | bytes 995336 | tf_op jit(solution)/shard_map/ppermute | solution.py:25
  21.2 0.0 copy-done.2
  21.2 1.1 %early_kernel.1 = (f32[8,128]{1,0:T(8,128)S(1)}, f32[128,1152]{1,0:T(8,128)S(1)}, bf16[128,1152]{1,0:T(8,128)(2,1)S(1)}, bf16[128,1152]{1,0:T(8,128)(2,1)S(1)}) custom-call(f32[1]{0:T(128)S(6)} %copy.7.log_scale, f32[1]{0:T(128)S(6)} %copy.8.logit_bias, s32[6]{0:T(128)S(1)} %stack.27.places, f32[64,1152]{1,0:T(8,128)S(1)} %copy-done.2, ...), custom_call_target="tpu_custom_call" | custom-call | flops 20384317440 | bytes 7077888 | tf_op jit(solution)/shard_map/early_kernel/pallas_call | solution.py:273
  22.3 11.1 %collective-permute-done.4.u2 = f32[64,1152]{1,0:T(8,128)S(1)} collective-permute-done((f32[64,1152]{1,0:T(8,128)S(1)}, f32[64,1152]{1,0:T(8,128)S(1)}, u32[]{:S(2)}, u32[]{:S(2)}) %collective-permute-start.4) | collective-permute-done | bytes 294944 | tf_op jit(solution)/shard_map/ppermute | solution.py:19
  33.5 0.1 late_kernel.1
  33.6 1.9 %collective-permute-start.5 = (f32[192,1152]{1,0:T(8,128)S(1)}, f32[192,1152]{1,0:T(8,128)S(1)}, u32[]{:S(2)}, u32[]{:S(2)}) collective-permute-start(f32[192,1152]{1,0:T(8,128)S(1)} %get-tuple-element.36), channel_id=1, source_target_pairs={{0,1},{1,0},{2,3},{3,2},{4,5},{5,4},{6,7},{7,6},{8,9},{9,8},{10,11... | collective-permute-start | bytes 2654216 | tf_op jit(solution)/shard_map/ppermute | solution.py:30
  35.5 0.0 collective-permute-done.3.p3
  35.6 0.0 collective-permute-done.2.p2
  35.6 2.1 %own_kernel.1 = (bf16[256,1152]{1,0:T(8,128)(2,1)S(1)}, bf16[256,1152]{1,0:T(8,128)(2,1)S(1)}, f32[8,256]{1,0:T(8,128)S(1)}, bf16[192,256]{1,0:T(8,128)(2,1)S(1)...) custom-call(f32[8,128]{1,0:T(8,128)S(1)} %get-tuple-element.28.scalars, f32[72,1152]{1,0:T(8,128)S(1)} %pack_kernel.1.p0, ...), custom_call_target="tpu_custom_call" | custom-call | flops 20384317440 | bytes 7077888 | tf_op jit(solution)/shard_map/own_kernel/pallas_call | solution.py:291
  37.7 0.2 collective-permute-done.5.units
  37.9 2.0 %cross_kernel.1 = (bf16[192,1152]{1,0:T(8,128)(2,1)S(1)}, bf16[192,1152]{1,0:T(8,128)(2,1)S(1)}, bf16[192,256]{1,0:T(8,128)(2,1)S(1)}, bf16[192,256]{1,0:T(8,128)(2,1)S(1)}, f32[192,1152]{1,0:T(8,128)S(1)}) custom-call(f32[8,128]{1,0:T(8,128)S(1)} %get-tuple-element.28.scalars, f32[192,1152]{1,0:T(8,128)S(1)} %collective-permute-done.5.units, ...), custom_call_target="tpu_custom_call" | custom-call | flops 679477248 | bytes 7077888 | tf_op jit(solution)/shard_map/cross_kernel/pallas_call | solution.py:297
  39.9 2.2 %collective-permute-start.6 = (f32[192,1152]{1,0:T(8,128)S(1)}, f32[192,1152]{1,0:T(8,128)S(1)}, u32[]{:S(2)}, u32[]{:S(2)}) collective-permute-start(f32[192,1152]{1,0:T(8,128)S(1)} %get-tuple-element.46), channel_id=1, source_target_pairs={{0,1},{1,0},{2,3},{3,2},{4,5},{5,4},{6,7},{7,6},{8,9},{9,8},{10,11... | collective-permute-start | bytes 2654216 | tf_op jit(solution)/shard_map/ppermute | solution.py:30
  42.1 1.2 %image_kernel.1 = (f32[64,1152]{1,0:T(8,128)S(1)}, f32[64,1152]{1,0:T(8,128)S(1)}, f32[64,1152]{1,0:T(8,128)S(1)}, f32[64,1152]{1,0:T(8,128)S(1)}) custom-call(bf16[192,256]{1,0:T(8,128)(2,1)S(1)} %get-tuple-element.34.w_high, bf16[192,256]{1,0:T(8,128)(2,1)S(1)} %get-tuple-element.35.w_low, bf16[192,1152]{1,0:T(8,128)(2,1)S(1)} %get-tuple-element.32.t_high, ...), custom_call_target="tpu_custom_call" | custom-call | flops 679477248 | bytes 7077888 | tf_op jit(solution)/shard_map/image_kernel/pallas_call | solution.py:301
  43.3 0.9 %collective-permute-done.6.other = f32[192,1152]{1,0:T(8,128)S(1)} collective-permute-done((f32[192,1152]{1,0:T(8,128)S(1)}, f32[192,1152]{1,0:T(8,128)S(1)}, u32[]{:S(2)}, u32[]{:S(2)}) %collective-permute-start.6) | collective-permute-done | bytes 884768 | tf_op jit(solution)/shard_map/ppermute | solution.py:30
  44.2 0.1 last_kernel.1
  44.3 7.0 %collective-permute-start.7 = (f32[64,1152]{1,0:T(8,128)S(1)}, f32[64,1152]{1,0:T(8,128)S(1)}, u32[]{:S(2)}, u32[]{:S(2)}) collective-permute-start(f32[64,1152]{1,0:T(8,128)S(1)} %get-tuple-element.48), channel_id=1, source_target_pairs={{0,760},{8,0},{16,8},{24,16},{32,24},{40,32},{48,40},{56,48},{64,5... | collective-permute-start | bytes 884744 | tf_op jit(solution)/shard_map/ppermute | solution.py:19
  51.2 4.7 %collective-permute-start.8 = (f32[64,1152]{1,0:T(8,128)S(1)}, f32[64,1152]{1,0:T(8,128)S(1)}, u32[]{:S(2)}, u32[]{:S(2)}) collective-permute-start(f32[64,1152]{1,0:T(8,128)S(1)} %get-tuple-element.49), channel_id=1, source_target_pairs={{0,6},{1,3},{2,0},{3,5},{4,2},{5,7},{6,4},{7,1},{8,14},{9,11},{10,... | collective-permute-start | bytes 884744 | tf_op jit(solution)/shard_map/ppermute | solution.py:25
  55.9 1.9 %collective-permute-start.10 = (f32[64,1152]{1,0:T(8,128)S(1)}, f32[64,1152]{1,0:T(8,128)S(1)}, u32[]{:S(2)}, u32[]{:S(2)}) collective-permute-start(f32[64,1152]{1,0:T(8,128)S(1)} %get-tuple-element.52), channel_id=1, source_target_pairs={{0,2},{1,7},{2,4},{3,1},{4,6},{5,3},{6,0},{7,5},{8,10},{9,15},{10,... | collective-permute-start | bytes 884744 | tf_op jit(solution)/shard_map/ppermute | solution.py:25
  57.8 0.1 collective-permute-done.7.back
  57.9 4.2 %collective-permute-done.8.moved = f32[64,1152]{1,0:T(8,128)S(1)} collective-permute-done((f32[64,1152]{1,0:T(8,128)S(1)}, f32[64,1152]{1,0:T(8,128)S(1)}, u32[]{:S(2)}, u32[]{:S(2)}) %collective-permute-start.8) | collective-permute-done | bytes 294944 | tf_op jit(solution)/shard_map/ppermute | solution.py:25
  62.1 0.0 copy-start.1
  62.1 0.1 middle_kernel.1
  62.2 5.6 %collective-permute-start.9 = (f32[64,1152]{1,0:T(8,128)S(1)}, f32[64,1152]{1,0:T(8,128)S(1)}, u32[]{:S(2)}, u32[]{:S(2)}) collective-permute-start(f32[64,1152]{1,0:T(8,128)S(1)} %get-tuple-element.51), channel_id=1, source_target_pairs={{0,6},{1,3},{2,0},{3,5},{4,2},{5,7},{6,4},{7,1},{8,14},{9,11},{10,... | collective-permute-start | bytes 884744 | tf_op jit(solution)/shard_map/ppermute | solution.py:25
  67.9 1.9 %collective-permute-start.11 = (f32[64,1152]{1,0:T(8,128)S(1)}, f32[64,1152]{1,0:T(8,128)S(1)}, u32[]{:S(2)}, u32[]{:S(2)}) collective-permute-start(f32[64,1152]{1,0:T(8,128)S(1)} %get-tuple-element.53), channel_id=1, source_target_pairs={{0,760},{8,0},{16,8},{24,16},{32,24},{40,32},{48,40},{56,48},{64,5... | collective-permute-start | bytes 884744 | tf_op jit(solution)/shard_map/ppermute | solution.py:19
  69.8 0.0 collective-permute-done.10.i3
  69.8 2.3 %collective-permute-done.9.i1 = f32[64,1152]{1,0:T(8,128)S(1)} collective-permute-done((f32[64,1152]{1,0:T(8,128)S(1)}, f32[64,1152]{1,0:T(8,128)S(1)}, u32[]{:S(2)}, u32[]{:S(2)}) %collective-permute-start.9) | collective-permute-done | bytes 294944 | tf_op jit(solution)/shard_map/ppermute | solution.py:25
  72.1 4.4 %collective-permute-done.11.back = f32[64,1152]{1,0:T(8,128)S(1)} collective-permute-done((f32[64,1152]{1,0:T(8,128)S(1)}, f32[64,1152]{1,0:T(8,128)S(1)}, u32[]{:S(2)}, u32[]{:S(2)}) %collective-permute-start.11) | collective-permute-done | bytes 294944 | tf_op jit(solution)/shard_map/ppermute | solution.py:19
  76.5 0.0 copy-done.1
  76.5 1.1 %finish.1 = (f32[64,1152]{1,0:T(8,128)}, f32[64,1152]{1,0:T(8,128)}) custom-call(f32[8,128]{1,0:T(8,128)S(1)} %get-tuple-element.28.scalars, f32[64,1152]{1,0:T(8,128)S(1)} %copy-done.1, f32[64,1152]{1,0:T(8,128)S(1)} %copy-done.2, f32[64,1152]{1,0:T(8,128)S(1)} %get-tuple-element.44.i0, f32[64,1152]{1,0:T(8,128)S(1)} %collective-permute-done.9.i1, ...), custom_call_target="tpu_custom_call" | custom-call | tf_op jit(solution)/shard_map/finish/pallas_call | solution.py:323
Async XLA Ops:
  0.6 4.3 %copy-start.3 = (s32[64]{0:T(128)S(1)}, s32[64]{0:T(128)}, u32[]{:S(2)}) copy-start(s32[64]{0:T(128)} %param.7) | copy-start | bytes 772
  0.6 15.5 %collective-permute-start = (f32[64,1152]{1,0:T(8,128)}, f32[64,1152]{1,0:T(8,128)S(1)}, u32[]{:S(2)}, u32[]{:S(2)}) collective-permute-start(f32[64,1152]{1,0:T(8,128)} %captions.1), channel_id=1, source_target_pairs={{0,8},{8,16},{16,24},{24,32},{32,40},{40,48},{48,56},{56,64},{64,7... | collective-permute-start | bytes 884744 | tf_op jit(solution)/shard_map/ppermute | solution.py:19
  4.9 1.0 %copy-start = (f32[64,1152]{1,0:T(8,128)S(1)}, f32[64,1152]{1,0:T(8,128)}, u32[]{:S(2)}) copy-start(f32[64,1152]{1,0:T(8,128)} %images.3) | copy-start | bytes 884740
  6.1 12.9 %collective-permute-start.1 = (f32[72,1152]{1,0:T(8,128)S(1)}, f32[72,1152]{1,0:T(8,128)S(1)}, u32[]{:S(2)}, u32[]{:S(2)}) collective-permute-start(f32[72,1152]{1,0:T(8,128)S(1)} %pack_kernel.1.p0), channel_id=1, source_target_pairs={{0,2},{1,7},{2,4},{3,1},{4,6},{5,3},{6,0},{7,5},{8,10},{9,15},{10,... | collective-permute-start | bytes 995336 | tf_op jit(solution)/shard_map/ppermute | solution.py:25
  9.5 26.1 %collective-permute-start.3 = (f32[72,1152]{1,0:T(8,128)S(1)}, f32[72,1152]{1,0:T(8,128)S(1)}, u32[]{:S(2)}, u32[]{:S(2)}) collective-permute-start(f32[72,1152]{1,0:T(8,128)S(1)} %pack_kernel.1.p0), channel_id=1, source_target_pairs={{0,6},{1,3},{2,0},{3,5},{4,2},{5,7},{6,4},{7,1},{8,14},{9,11},{10,... | collective-permute-start | bytes 995336 | tf_op jit(solution)/shard_map/ppermute | solution.py:25
  14.6 6.6 %copy-start.2 = (f32[64,1152]{1,0:T(8,128)S(1)}, f32[64,1152]{1,0:T(8,128)}, u32[]{:S(2)}) copy-start(f32[64,1152]{1,0:T(8,128)} %captions.1) | copy-start | bytes 884740
  16.2 17.2 %collective-permute-start.4 = (f32[64,1152]{1,0:T(8,128)S(1)}, f32[64,1152]{1,0:T(8,128)S(1)}, u32[]{:S(2)}, u32[]{:S(2)}) collective-permute-start(f32[64,1152]{1,0:T(8,128)S(1)} %unit_kernel.1.u1), channel_id=1, source_target_pairs={{0,8},{8,16},{16,24},{24,32},{32,40},{40,48},{48,56},{56,64},{64,7... | collective-permute-start | bytes 884744 | tf_op jit(solution)/shard_map/ppermute | solution.py:19
  19.0 16.6 %collective-permute-start.2 = (f32[72,1152]{1,0:T(8,128)S(1)}, f32[72,1152]{1,0:T(8,128)S(1)}, u32[]{:S(2)}, u32[]{:S(2)}) collective-permute-start(f32[72,1152]{1,0:T(8,128)S(1)} %collective-permute-done.1.p1), channel_id=1, source_target_pairs={{0,2},{1,7},{2,4},{3,1},{4,6},{5,3},{6,0},{7,5},{8,10},{9,15},{10,... | collective-permute-start | bytes 995336 | tf_op jit(solution)/shard_map/ppermute | solution.py:25
  33.6 4.3 %collective-permute-start.5 = (f32[192,1152]{1,0:T(8,128)S(1)}, f32[192,1152]{1,0:T(8,128)S(1)}, u32[]{:S(2)}, u32[]{:S(2)}) collective-permute-start(f32[192,1152]{1,0:T(8,128)S(1)} %get-tuple-element.36), channel_id=1, source_target_pairs={{0,1},{1,0},{2,3},{3,2},{4,5},{5,4},{6,7},{7,6},{8,9},{9,8},{10,11... | collective-permute-start | bytes 2654216 | tf_op jit(solution)/shard_map/ppermute | solution.py:30
  39.9 4.3 %collective-permute-start.6 = (f32[192,1152]{1,0:T(8,128)S(1)}, f32[192,1152]{1,0:T(8,128)S(1)}, u32[]{:S(2)}, u32[]{:S(2)}) collective-permute-start(f32[192,1152]{1,0:T(8,128)S(1)} %get-tuple-element.46), channel_id=1, source_target_pairs={{0,1},{1,0},{2,3},{3,2},{4,5},{5,4},{6,7},{7,6},{8,9},{9,8},{10,11... | collective-permute-start | bytes 2654216 | tf_op jit(solution)/shard_map/ppermute | solution.py:30
  44.3 13.7 %collective-permute-start.7 = (f32[64,1152]{1,0:T(8,128)S(1)}, f32[64,1152]{1,0:T(8,128)S(1)}, u32[]{:S(2)}, u32[]{:S(2)}) collective-permute-start(f32[64,1152]{1,0:T(8,128)S(1)} %get-tuple-element.48), channel_id=1, source_target_pairs={{0,760},{8,0},{16,8},{24,16},{32,24},{40,32},{48,40},{56,48},{64,5... | collective-permute-start | bytes 884744 | tf_op jit(solution)/shard_map/ppermute | solution.py:19
  51.2 10.9 %collective-permute-start.8 = (f32[64,1152]{1,0:T(8,128)S(1)}, f32[64,1152]{1,0:T(8,128)S(1)}, u32[]{:S(2)}, u32[]{:S(2)}) collective-permute-start(f32[64,1152]{1,0:T(8,128)S(1)} %get-tuple-element.49), channel_id=1, source_target_pairs={{0,6},{1,3},{2,0},{3,5},{4,2},{5,7},{6,4},{7,1},{8,14},{9,11},{10,... | collective-permute-start | bytes 884744 | tf_op jit(solution)/shard_map/ppermute | solution.py:25
  55.9 13.9 %collective-permute-start.10 = (f32[64,1152]{1,0:T(8,128)S(1)}, f32[64,1152]{1,0:T(8,128)S(1)}, u32[]{:S(2)}, u32[]{:S(2)}) collective-permute-start(f32[64,1152]{1,0:T(8,128)S(1)} %get-tuple-element.52), channel_id=1, source_target_pairs={{0,2},{1,7},{2,4},{3,1},{4,6},{5,3},{6,0},{7,5},{8,10},{9,15},{10,... | collective-permute-start | bytes 884744 | tf_op jit(solution)/shard_map/ppermute | solution.py:25
  62.1 14.3 %copy-start.1 = (f32[64,1152]{1,0:T(8,128)S(1)}, f32[64,1152]{1,0:T(8,128)}, u32[]{:S(2)}) copy-start(f32[64,1152]{1,0:T(8,128)} %images.3) | copy-start | bytes 884740
  62.2 9.8 %collective-permute-start.9 = (f32[64,1152]{1,0:T(8,128)S(1)}, f32[64,1152]{1,0:T(8,128)S(1)}, u32[]{:S(2)}, u32[]{:S(2)}) collective-permute-start(f32[64,1152]{1,0:T(8,128)S(1)} %get-tuple-element.51), channel_id=1, source_target_pairs={{0,6},{1,3},{2,0},{3,5},{4,2},{5,7},{6,4},{7,1},{8,14},{9,11},{10,... | collective-permute-start | bytes 884744 | tf_op jit(solution)/shard_map/ppermute | solution.py:25
  67.9 8.6 %collective-permute-start.11 = (f32[64,1152]{1,0:T(8,128)S(1)}, f32[64,1152]{1,0:T(8,128)S(1)}, u32[]{:S(2)}, u32[]{:S(2)}) collective-permute-start(f32[64,1152]{1,0:T(8,128)S(1)} %get-tuple-element.53), channel_id=1, source_target_pairs={{0,760},{8,0},{16,8},{24,16},{32,24},{40,32},{48,40},{56,48},{64,5... | collective-permute-start | bytes 884744 | tf_op jit(solution)/shard_map/ppermute | solution.py:19

commit v4 on v3

--- a/solution.py
+++ b/solution.py
@@ -170,15 +170,13 @@
         out[...] = total[k * ROWS : (k + 1) * ROWS, :]
 
 
-def last_kernel(own, other, image_part, out, passed):
-    at = (WIN - 1) * ROWS
-    out[...] = own[at:, :] + other[at:, :]
-    passed[...] = image_part[...]
-
-
-def middle_kernel(back, moved, own, other, part, out_text, out_image):
-    out_text[...] = (own[ROWS : 2 * ROWS, :] + other[ROWS : 2 * ROWS, :]) + back[...]
-    out_image[...] = part[...] + moved[...]
+def last_kernel(own, other, after, out1, out2):
+    out1[...] = own[ROWS : 2 * ROWS, :] + other[ROWS : 2 * ROWS, :]
+    out2[...] = own[2 * ROWS :, :] + other[2 * ROWS :, :]
+
+
+def sum_kernel(own, other, back1, back2, out):
+    out[...] = (own[:ROWS, :] + other[:ROWS, :]) + (back1[...] + back2[...])
 
 
 def finish(values, grad, temper):
@@ -190,14 +188,13 @@
 
 
 def final_kernel(
-    scalars, images, captions, i0, i1, i3, own, other, back, out_images, out_captions
+    scalars, images, captions, grad_text, i0, i2, i1, i3, out_images, out_captions
 ):
     temper = scalars[0:1, 0:1]
     for r in range(0, ROWS, 32):
         at = slice(r, r + 32)
-        grad = (own[at, :] + other[at, :]) + back[at, :]
-        out_captions[at, :] = finish(captions[at, :], grad, temper)
-        grad = (i0[at, :] + i1[at, :]) + i3[at, :]
+        out_captions[at, :] = finish(captions[at, :], grad_text[at, :], temper)
+        grad = (i0[at, :] + i2[at, :]) + (i1[at, :] + i3[at, :])
         out_images[at, :] = finish(images[at, :], grad, temper)
 
 
@@ -301,21 +298,19 @@
     i0, i1, i2, i3 = call(image_kernel, 8, [f32(ROWS, D)] * X, 2)(
         w_high, w_low, t_high, t_low, ow_high, ow_low, ot_high, ot_low
     )
-    back, i2 = pl.pallas_call(
+    back1, back2 = pl.pallas_call(
         last_kernel,
-        in_specs=[VMEM] * 3,
+        in_specs=[VMEM, VMEM, HBM],
         out_specs=[VMEM] * 2,
         out_shape=[f32(ROWS, D)] * 2,
         compiler_params=pltpu.CompilerParams(vmem_limit_bytes=VMEM_LIMIT),
         name="last_kernel",
-    )(own_text, other_text, i2)
-    back = along_loop(back, -1)
-    moved = along_x(i2, -1)
-    back, i1 = call(middle_kernel, 5, [f32(ROWS, D)] * 2, 0)(
-        back, moved, own_text, other_text, i1
-    )
+    )(own_text, other_text, i0)
+    back2 = along_loop(back2, -2)
+    back1 = along_loop(back1, -1)
+    (grad_text,) = call(sum_kernel, 4, [f32(ROWS, D)], 1)(own_text, other_text, back1, back2)
+    i2 = along_x(i2, 2)
     i1 = along_x(i1, -1)
-    back = along_loop(back, -1)
     i3 = along_x(i3, 1)
 
     first = pl.BlockSpec((ROWS, D), lambda i: (0, 0))
@@ -323,12 +318,12 @@
         pl.pallas_call(
             final_kernel,
             grid=(1,),
-            in_specs=[pl.BlockSpec((8, 128), lambda i: (0, 0))] + [first] * 8,
+            in_specs=[pl.BlockSpec((8, 128), lambda i: (0, 0))] + [first] * 7,
             out_specs=[first] * 2,
             out_shape=[f32(ROWS, D)] * 2,
             compiler_params=pltpu.CompilerParams(vmem_limit_bytes=VMEM_LIMIT),
             name="finish",
-        )(scalars, images, captions, i0, i1, i3, own_text, other_text, back)
+        )(scalars, images, captions, grad_text, i0, i2, i1, i3)
     )
 
 

time: 78 us -> 75.4 us (0.967)
  the two profiles are of different devices: /device:TPU:64 before, /device:TPU:1 now
where the time goes in v4:
time: 75.4 us; the launch traced here: 74.9 us
  starting transfers between devices  39 us (52%)
  waiting for transfers between devices  24.6 us (33%)
  Pallas kernels  8.06 us (11%)
  between operations  2.22 us (3%)
  local copies, waits for them, and re-layouts  1.05 us (1%)
    ppermute x4, waiting for transfers between devices, along_loop(): lax.ppermute(shard, 'loop', [(i, (i + by) % count) for i in range(count)])  21.9 us
    ppermute x6, starting transfers between devices, along_x(): return lax.ppermute(shard, 'group', pairs)  20.6 us
    ppermute x4, starting transfers between devices, along_loop(): lax.ppermute(shard, 'loop', [(i, (i + by) % count) for i in range(count)])  12.2 us
    ppermute x2, starting transfers between devices, across_cores(): return lax.ppermute(shard, 'group', [(i, i ^ 1) for i in range(count)])  6.2 us
    pallas_call x1, Pallas kernels, per_device(): call(own_kernel, 7, image_halves + [f32(8, images_all)] + weight_halves +...  2.13 us
    pallas_call x1, Pallas kernels, per_device(): call(cross_kernel, 5, text_halves + weight_halves + [f32(texts_all, D)], 2)  1.96 us
    ppermute x6, waiting for transfers between devices, along_x(): return lax.ppermute(shard, 'group', pairs)  1.78 us
  transfers between devices with their start and end apart: 12, of which 5 were waited for; matrix products, arithmetic and copies ran while one was open for 0% of the time, Pallas kernels for 7%

profile of v4, /device:TPU:1, one launch (start us, length us, event | category | flops | bytes accessed | tf_op | source)
XLA Modules:
  0.0 74.9 jit_solution(16492918877010382328)
XLA Ops:
  0.6 0.0 copy-start.3
  0.6 4.8 %collective-permute-start = (f32[64,1152]{1,0:T(8,128)}, f32[64,1152]{1,0:T(8,128)S(1)}, u32[]{:S(2)}, u32[]{:S(2)}) collective-permute-start(f32[64,1152]{1,0:T(8,128)} %captions.1), channel_id=1, source_target_pairs={{0,8},{8,16},{16,24},{24,32},{32,40},{40,48},{48,56},{56,64},{64,7... | collective-permute-start | bytes 884744 | tf_op jit(solution)/shard_map/ppermute | solution.py:19
  5.5 0.0 copy-done.3
  5.5 0.0 copy-start
  5.5 1.0 %copy-done = f32[64,1152]{1,0:T(8,128)S(1)} copy-done((f32[64,1152]{1,0:T(8,128)S(1)}, f32[64,1152]{1,0:T(8,128)}, u32[]{:S(2)}) %copy-start) | copy-done | bytes 294936
  6.5 0.2 pack_kernel.1.p0
  6.6 4.4 %collective-permute-start.1 = (f32[72,1152]{1,0:T(8,128)S(1)}, f32[72,1152]{1,0:T(8,128)S(1)}, u32[]{:S(2)}, u32[]{:S(2)}) collective-permute-start(f32[72,1152]{1,0:T(8,128)S(1)} %pack_kernel.1.p0), channel_id=1, source_target_pairs={{0,2},{1,7},{2,4},{3,1},{4,6},{5,3},{6,0},{7,5},{8,10},{9,15},{10,... | collective-permute-start | bytes 995336 | tf_op jit(solution)/shard_map/ppermute | solution.py:25
  11.0 1.9 %collective-permute-start.3 = (f32[72,1152]{1,0:T(8,128)S(1)}, f32[72,1152]{1,0:T(8,128)S(1)}, u32[]{:S(2)}, u32[]{:S(2)}) collective-permute-start(f32[72,1152]{1,0:T(8,128)S(1)} %pack_kernel.1.p0), channel_id=1, source_target_pairs={{0,6},{1,3},{2,0},{3,5},{4,2},{5,7},{6,4},{7,1},{8,14},{9,11},{10,... | collective-permute-start | bytes 995336 | tf_op jit(solution)/shard_map/ppermute | solution.py:25
  14.3 0.1 stack.27.places
  14.4 0.0 copy-start.2
  14.4 11.2 %collective-permute-done.text = f32[64,1152]{1,0:T(8,128)S(1)} collective-permute-done((f32[64,1152]{1,0:T(8,128)}, f32[64,1152]{1,0:T(8,128)S(1)}, u32[]{:S(2)}, u32[]{:S(2)}) %collective-permute-start) | collective-permute-done | bytes 294944 | tf_op jit(solution)/shard_map/ppermute | solution.py:19
  25.6 0.1 unit_kernel.1.u1
  25.7 1.9 %collective-permute-start.4 = (f32[64,1152]{1,0:T(8,128)S(1)}, f32[64,1152]{1,0:T(8,128)S(1)}, u32[]{:S(2)}, u32[]{:S(2)}) collective-permute-start(f32[64,1152]{1,0:T(8,128)S(1)} %unit_kernel.1.u1), channel_id=1, source_target_pairs={{0,8},{8,16},{16,24},{24,32},{32,40},{40,48},{48,56},{56,64},{64,7... | collective-permute-start | bytes 884744 | tf_op jit(solution)/shard_map/ppermute | solution.py:19
  27.7 0.0 collective-permute-done.1.p1
  27.7 4.4 %collective-permute-start.2 = (f32[72,1152]{1,0:T(8,128)S(1)}, f32[72,1152]{1,0:T(8,128)S(1)}, u32[]{:S(2)}, u32[]{:S(2)}) collective-permute-start(f32[72,1152]{1,0:T(8,128)S(1)} %collective-permute-done.1.p1), channel_id=1, source_target_pairs={{0,2},{1,7},{2,4},{3,1},{4,6},{5,3},{6,0},{7,5},{8,10},{9,15},{10,... | collective-permute-start | bytes 995336 | tf_op jit(solution)/shard_map/ppermute | solution.py:25
  32.1 0.0 copy-done.2
  32.1 1.1 %early_kernel.1 = (f32[8,128]{1,0:T(8,128)S(1)}, f32[128,1152]{1,0:T(8,128)S(1)}, bf16[128,1152]{1,0:T(8,128)(2,1)S(1)}, bf16[128,1152]{1,0:T(8,128)(2,1)S(1)}) custom-call(f32[1]{0:T(128)S(6)} %copy.7.log_scale, f32[1]{0:T(128)S(6)} %copy.8.logit_bias, s32[6]{0:T(128)S(1)} %stack.27.places, f32[64,1152]{1,0:T(8,128)S(1)} %copy-done.2, ...), custom_call_target="tpu_custom_call" | custom-call | flops 20384317440 | bytes 7077888 | tf_op jit(solution)/shard_map/early_kernel/pallas_call | solution.py:270
  33.2 5.0 %collective-permute-done.4.u2 = f32[64,1152]{1,0:T(8,128)S(1)} collective-permute-done((f32[64,1152]{1,0:T(8,128)S(1)}, f32[64,1152]{1,0:T(8,128)S(1)}, u32[]{:S(2)}, u32[]{:S(2)}) %collective-permute-start.4) | collective-permute-done | bytes 294944 | tf_op jit(solution)/shard_map/ppermute | solution.py:19
  38.2 0.1 late_kernel.1
  38.4 4.1 %collective-permute-start.5 = (f32[192,1152]{1,0:T(8,128)S(1)}, f32[192,1152]{1,0:T(8,128)S(1)}, u32[]{:S(2)}, u32[]{:S(2)}) collective-permute-start(f32[192,1152]{1,0:T(8,128)S(1)} %get-tuple-element.33), channel_id=1, source_target_pairs={{0,1},{1,0},{2,3},{3,2},{4,5},{5,4},{6,7},{7,6},{8,9},{9,8},{10,11... | collective-permute-start | bytes 2654216 | tf_op jit(solution)/shard_map/ppermute | solution.py:30
  42.4 0.0 collective-permute-done.3.p3
  42.4 0.0 collective-permute-done.2.p2
  42.5 2.1 %own_kernel.1 = (bf16[256,1152]{1,0:T(8,128)(2,1)S(1)}, bf16[256,1152]{1,0:T(8,128)(2,1)S(1)}, f32[8,256]{1,0:T(8,128)S(1)}, bf16[192,256]{1,0:T(8,128)(2,1)S(1)...) custom-call(f32[8,128]{1,0:T(8,128)S(1)} %get-tuple-element.26.scalars, f32[72,1152]{1,0:T(8,128)S(1)} %pack_kernel.1.p0, ...), custom_call_target="tpu_custom_call" | custom-call | flops 20384317440 | bytes 7077888 | tf_op jit(solution)/shard_map/own_kernel/pallas_call | solution.py:288
  44.6 0.0 collective-permute-done.5.units
  44.6 2.0 %cross_kernel.1 = (bf16[192,1152]{1,0:T(8,128)(2,1)S(1)}, bf16[192,1152]{1,0:T(8,128)(2,1)S(1)}, bf16[192,256]{1,0:T(8,128)(2,1)S(1)}, bf16[192,256]{1,0:T(8,128)(2,1)S(1)}, f32[192,1152]{1,0:T(8,128)S(1)}) custom-call(f32[8,128]{1,0:T(8,128)S(1)} %get-tuple-element.26.scalars, f32[192,1152]{1,0:T(8,128)S(1)} %collective-permute-done.5.units, ...), custom_call_target="tpu_custom_call" | custom-call | flops 679477248 | bytes 7077888 | tf_op jit(solution)/shard_map/cross_kernel/pallas_call | solution.py:294
  46.6 2.1 %collective-permute-start.6 = (f32[192,1152]{1,0:T(8,128)S(1)}, f32[192,1152]{1,0:T(8,128)S(1)}, u32[]{:S(2)}, u32[]{:S(2)}) collective-permute-start(f32[192,1152]{1,0:T(8,128)S(1)} %get-tuple-element.37), channel_id=1, source_target_pairs={{0,1},{1,0},{2,3},{3,2},{4,5},{5,4},{6,7},{7,6},{8,9},{9,8},{10,11... | collective-permute-start | bytes 2654216 | tf_op jit(solution)/shard_map/ppermute | solution.py:30
  48.7 1.2 %image_kernel.1 = (f32[64,1152]{1,0:T(8,128)S(1)}, f32[64,1152]{1,0:T(8,128)S(1)}, f32[64,1152]{1,0:T(8,128)S(1)}, f32[64,1152]{1,0:T(8,128)S(1)}) custom-call(bf16[192,256]{1,0:T(8,128)(2,1)S(1)} %get-tuple-element.38.w_high, bf16[192,256]{1,0:T(8,128)(2,1)S(1)} %get-tuple-element.39.w_low, bf16[192,1152]{1,0:T(8,128)(2,1)S(1)} %get-tuple-element.30.t_high, ...), custom_call_target="tpu_custom_call" | custom-call | flops 679477248 | bytes 7077888 | tf_op jit(solution)/shard_map/image_kernel/pallas_call | solution.py:298
  50.0 0.9 %collective-permute-done.6.other = f32[192,1152]{1,0:T(8,128)S(1)} collective-permute-done((f32[192,1152]{1,0:T(8,128)S(1)}, f32[192,1152]{1,0:T(8,128)S(1)}, u32[]{:S(2)}, u32[]{:S(2)}) %collective-permute-start.6) | collective-permute-done | bytes 884768 | tf_op jit(solution)/shard_map/ppermute | solution.py:30
  50.9 0.1 last_kernel.1
  51.0 3.2 %collective-permute-start.7 = (f32[64,1152]{1,0:T(8,128)S(1)}, f32[64,1152]{1,0:T(8,128)S(1)}, u32[]{:S(2)}, u32[]{:S(2)}) collective-permute-start(f32[64,1152]{1,0:T(8,128)S(1)} %get-tuple-element.45), channel_id=1, source_target_pairs={{0,760},{8,0},{16,8},{24,16},{32,24},{40,32},{48,40},{56,48},{64,5... | collective-permute-start | bytes 884744 | tf_op jit(solution)/shard_map/ppermute | solution.py:19
  54.2 2.2 %collective-permute-start.8 = (f32[64,1152]{1,0:T(8,128)S(1)}, f32[64,1152]{1,0:T(8,128)S(1)}, u32[]{:S(2)}, u32[]{:S(2)}) collective-permute-start(f32[64,1152]{1,0:T(8,128)S(1)} %get-tuple-element.46), channel_id=1, source_target_pairs={{0,752},{8,760},{16,0},{24,8},{32,16},{40,24},{48,32},{56,40},{64,... | collective-permute-start | bytes 884744 | tf_op jit(solution)/shard_map/ppermute | solution.py:19
  56.4 3.2 %collective-permute-start.9 = (f32[64,1152]{1,0:T(8,128)S(1)}, f32[64,1152]{1,0:T(8,128)S(1)}, u32[]{:S(2)}, u32[]{:S(2)}) collective-permute-start(f32[64,1152]{1,0:T(8,128)S(1)} %get-tuple-element.47), channel_id=1, source_target_pairs={{0,4},{1,5},{2,6},{3,7},{4,0},{5,1},{6,2},{7,3},{8,12},{9,13},{10,... | collective-permute-start | bytes 884744 | tf_op jit(solution)/shard_map/ppermute | solution.py:25
  59.7 2.3 %collective-permute-start.10 = (f32[64,1152]{1,0:T(8,128)S(1)}, f32[64,1152]{1,0:T(8,128)S(1)}, u32[]{:S(2)}, u32[]{:S(2)}) collective-permute-start(f32[64,1152]{1,0:T(8,128)S(1)} %get-tuple-element.48), channel_id=1, source_target_pairs={{0,6},{1,3},{2,0},{3,5},{4,2},{5,7},{6,4},{7,1},{8,14},{9,11},{10,... | collective-permute-start | bytes 884744 | tf_op jit(solution)/shard_map/ppermute | solution.py:25
  62.0 0.0 copy-start.1
  62.0 4.4 %collective-permute-start.11 = (f32[64,1152]{1,0:T(8,128)S(1)}, f32[64,1152]{1,0:T(8,128)S(1)}, u32[]{:S(2)}, u32[]{:S(2)}) collective-permute-start(f32[64,1152]{1,0:T(8,128)S(1)} %get-tuple-element.49), channel_id=1, source_target_pairs={{0,2},{1,7},{2,4},{3,1},{4,6},{5,3},{6,0},{7,5},{8,10},{9,15},{10,... | collective-permute-start | bytes 884744 | tf_op jit(solution)/shard_map/ppermute | solution.py:25
  66.4 0.0 collective-permute-done.7.back1
  66.4 5.6 %collective-permute-done.8.back2 = f32[64,1152]{1,0:T(8,128)S(1)} collective-permute-done((f32[64,1152]{1,0:T(8,128)S(1)}, f32[64,1152]{1,0:T(8,128)S(1)}, u32[]{:S(2)}, u32[]{:S(2)}) %collective-permute-start.8) | collective-permute-done | bytes 294944 | tf_op jit(solution)/shard_map/ppermute | solution.py:19
  72.0 0.1 sum_kernel.1.grad_text
  72.0 0.0 collective-permute-done.9.i2
  72.0 1.8 %collective-permute-done.10.i1 = f32[64,1152]{1,0:T(8,128)S(1)} collective-permute-done((f32[64,1152]{1,0:T(8,128)S(1)}, f32[64,1152]{1,0:T(8,128)S(1)}, u32[]{:S(2)}, u32[]{:S(2)}) %collective-permute-start.10) | collective-permute-done | bytes 294944 | tf_op jit(solution)/shard_map/ppermute | solution.py:25
  73.8 0.0 collective-permute-done.11.i3
  73.8 0.0 copy-done.1
  73.8 1.1 %finish.1 = (f32[64,1152]{1,0:T(8,128)}, f32[64,1152]{1,0:T(8,128)}) custom-call(f32[8,128]{1,0:T(8,128)S(1)} %get-tuple-element.26.scalars, f32[64,1152]{1,0:T(8,128)S(1)} %copy-done.1, f32[64,1152]{1,0:T(8,128)S(1)} %copy-done.2, f32[64,1152]{1,0:T(8,128)S(1)} %sum_kernel.1.grad_text, f32[64,1152]{1,0:T(8,128)S(1)} %get-tuple-element.44.after.i0, ...), custom_call_target="tpu_custom_call" | custom-call | tf_op jit(solution)/shard_map/finish/pallas_call | solution.py:318
Async XLA Ops:
  0.6 4.9 %copy-start.3 = (s32[64]{0:T(128)S(1)}, s32[64]{0:T(128)}, u32[]{:S(2)}) copy-start(s32[64]{0:T(128)} %param.7) | copy-start | bytes 772
  0.6 25.0 %collective-permute-start = (f32[64,1152]{1,0:T(8,128)}, f32[64,1152]{1,0:T(8,128)S(1)}, u32[]{:S(2)}, u32[]{:S(2)}) collective-permute-start(f32[64,1152]{1,0:T(8,128)} %captions.1), channel_id=1, source_target_pairs={{0,8},{8,16},{16,24},{24,32},{32,40},{40,48},{48,56},{56,64},{64,7... | collective-permute-start | bytes 884744 | tf_op jit(solution)/shard_map/ppermute | solution.py:19
  5.5 1.0 %copy-start = (f32[64,1152]{1,0:T(8,128)S(1)}, f32[64,1152]{1,0:T(8,128)}, u32[]{:S(2)}) copy-start(f32[64,1152]{1,0:T(8,128)} %images.3) | copy-start | bytes 884740
  6.6 21.1 %collective-permute-start.1 = (f32[72,1152]{1,0:T(8,128)S(1)}, f32[72,1152]{1,0:T(8,128)S(1)}, u32[]{:S(2)}, u32[]{:S(2)}) collective-permute-start(f32[72,1152]{1,0:T(8,128)S(1)} %pack_kernel.1.p0), channel_id=1, source_target_pairs={{0,2},{1,7},{2,4},{3,1},{4,6},{5,3},{6,0},{7,5},{8,10},{9,15},{10,... | collective-permute-start | bytes 995336 | tf_op jit(solution)/shard_map/ppermute | solution.py:25
  11.0 31.4 %collective-permute-start.3 = (f32[72,1152]{1,0:T(8,128)S(1)}, f32[72,1152]{1,0:T(8,128)S(1)}, u32[]{:S(2)}, u32[]{:S(2)}) collective-permute-start(f32[72,1152]{1,0:T(8,128)S(1)} %pack_kernel.1.p0), channel_id=1, source_target_pairs={{0,6},{1,3},{2,0},{3,5},{4,2},{5,7},{6,4},{7,1},{8,14},{9,11},{10,... | collective-permute-start | bytes 995336 | tf_op jit(solution)/shard_map/ppermute | solution.py:25
  14.4 17.7 %copy-start.2 = (f32[64,1152]{1,0:T(8,128)S(1)}, f32[64,1152]{1,0:T(8,128)}, u32[]{:S(2)}) copy-start(f32[64,1152]{1,0:T(8,128)} %captions.1) | copy-start | bytes 884740
  25.7 12.5 %collective-permute-start.4 = (f32[64,1152]{1,0:T(8,128)S(1)}, f32[64,1152]{1,0:T(8,128)S(1)}, u32[]{:S(2)}, u32[]{:S(2)}) collective-permute-start(f32[64,1152]{1,0:T(8,128)S(1)} %unit_kernel.1.u1), channel_id=1, source_target_pairs={{0,8},{8,16},{16,24},{24,32},{32,40},{40,48},{48,56},{56,64},{64,7... | collective-permute-start | bytes 884744 | tf_op jit(solution)/shard_map/ppermute | solution.py:19
  27.7 14.8 %collective-permute-start.2 = (f32[72,1152]{1,0:T(8,128)S(1)}, f32[72,1152]{1,0:T(8,128)S(1)}, u32[]{:S(2)}, u32[]{:S(2)}) collective-permute-start(f32[72,1152]{1,0:T(8,128)S(1)} %collective-permute-done.1.p1), channel_id=1, source_target_pairs={{0,2},{1,7},{2,4},{3,1},{4,6},{5,3},{6,0},{7,5},{8,10},{9,15},{10,... | collective-permute-start | bytes 995336 | tf_op jit(solution)/shard_map/ppermute | solution.py:25
  38.4 6.2 %collective-permute-start.5 = (f32[192,1152]{1,0:T(8,128)S(1)}, f32[192,1152]{1,0:T(8,128)S(1)}, u32[]{:S(2)}, u32[]{:S(2)}) collective-permute-start(f32[192,1152]{1,0:T(8,128)S(1)} %get-tuple-element.33), channel_id=1, source_target_pairs={{0,1},{1,0},{2,3},{3,2},{4,5},{5,4},{6,7},{7,6},{8,9},{9,8},{10,11... | collective-permute-start | bytes 2654216 | tf_op jit(solution)/shard_map/ppermute | solution.py:30
  46.6 4.3 %collective-permute-start.6 = (f32[192,1152]{1,0:T(8,128)S(1)}, f32[192,1152]{1,0:T(8,128)S(1)}, u32[]{:S(2)}, u32[]{:S(2)}) collective-permute-start(f32[192,1152]{1,0:T(8,128)S(1)} %get-tuple-element.37), channel_id=1, source_target_pairs={{0,1},{1,0},{2,3},{3,2},{4,5},{5,4},{6,7},{7,6},{8,9},{9,8},{10,11... | collective-permute-start | bytes 2654216 | tf_op jit(solution)/shard_map/ppermute | solution.py:30
  51.0 15.4 %collective-permute-start.7 = (f32[64,1152]{1,0:T(8,128)S(1)}, f32[64,1152]{1,0:T(8,128)S(1)}, u32[]{:S(2)}, u32[]{:S(2)}) collective-permute-start(f32[64,1152]{1,0:T(8,128)S(1)} %get-tuple-element.45), channel_id=1, source_target_pairs={{0,760},{8,0},{16,8},{24,16},{32,24},{40,32},{48,40},{56,48},{64,5... | collective-permute-start | bytes 884744 | tf_op jit(solution)/shard_map/ppermute | solution.py:19
  54.2 17.8 %collective-permute-start.8 = (f32[64,1152]{1,0:T(8,128)S(1)}, f32[64,1152]{1,0:T(8,128)S(1)}, u32[]{:S(2)}, u32[]{:S(2)}) collective-permute-start(f32[64,1152]{1,0:T(8,128)S(1)} %get-tuple-element.46), channel_id=1, source_target_pairs={{0,752},{8,760},{16,0},{24,8},{32,16},{40,24},{48,32},{56,40},{64,... | collective-permute-start | bytes 884744 | tf_op jit(solution)/shard_map/ppermute | solution.py:19
  56.4 15.6 %collective-permute-start.9 = (f32[64,1152]{1,0:T(8,128)S(1)}, f32[64,1152]{1,0:T(8,128)S(1)}, u32[]{:S(2)}, u32[]{:S(2)}) collective-permute-start(f32[64,1152]{1,0:T(8,128)S(1)} %get-tuple-element.47), channel_id=1, source_target_pairs={{0,4},{1,5},{2,6},{3,7},{4,0},{5,1},{6,2},{7,3},{8,12},{9,13},{10,... | collective-permute-start | bytes 884744 | tf_op jit(solution)/shard_map/ppermute | solution.py:25
  59.7 14.1 %collective-permute-start.10 = (f32[64,1152]{1,0:T(8,128)S(1)}, f32[64,1152]{1,0:T(8,128)S(1)}, u32[]{:S(2)}, u32[]{:S(2)}) collective-permute-start(f32[64,1152]{1,0:T(8,128)S(1)} %get-tuple-element.48), channel_id=1, source_target_pairs={{0,6},{1,3},{2,0},{3,5},{4,2},{5,7},{6,4},{7,1},{8,14},{9,11},{10,... | collective-permute-start | bytes 884744 | tf_op jit(solution)/shard_map/ppermute | solution.py:25
  62.0 11.8 %copy-start.1 = (f32[64,1152]{1,0:T(8,128)S(1)}, f32[64,1152]{1,0:T(8,128)}, u32[]{:S(2)}) copy-start(f32[64,1152]{1,0:T(8,128)} %images.3) | copy-start | bytes 884740
  62.0 11.8 %collective-permute-start.11 = (f32[64,1152]{1,0:T(8,128)S(1)}, f32[64,1152]{1,0:T(8,128)S(1)}, u32[]{:S(2)}, u32[]{:S(2)}) collective-permute-start(f32[64,1152]{1,0:T(8,128)S(1)} %get-tuple-element.49), channel_id=1, source_target_pairs={{0,2},{1,7},{2,4},{3,1},{4,6},{5,3},{6,0},{7,5},{8,10},{9,15},{10,... | collective-permute-start | bytes 884744 | tf_op jit(solution)/shard_map/ppermute | solution.py:25

commit v5 on v4

--- a/solution.py
+++ b/solution.py
@@ -175,6 +175,10 @@
     out2[...] = own[2 * ROWS :, :] + other[2 * ROWS :, :]
 
 
+def add_kernel(a, b, out):
+    out[...] = a[...] + b[...]
+
+
 def sum_kernel(own, other, back1, back2, out):
     out[...] = (own[:ROWS, :] + other[:ROWS, :]) + (back1[...] + back2[...])
 
@@ -188,13 +192,13 @@
 
 
 def final_kernel(
-    scalars, images, captions, grad_text, i0, i2, i1, i3, out_images, out_captions
+    scalars, images, captions, i0, i1, i3, grad_text, out_images, out_captions
 ):
     temper = scalars[0:1, 0:1]
     for r in range(0, ROWS, 32):
         at = slice(r, r + 32)
         out_captions[at, :] = finish(captions[at, :], grad_text[at, :], temper)
-        grad = (i0[at, :] + i2[at, :]) + (i1[at, :] + i3[at, :])
+        grad = (i0[at, :] + i1[at, :]) + i3[at, :]
         out_images[at, :] = finish(images[at, :], grad, temper)
 
 
@@ -308,8 +312,8 @@
     )(own_text, other_text, i0)
     back2 = along_loop(back2, -2)
     back1 = along_loop(back1, -1)
-    (grad_text,) = call(sum_kernel, 4, [f32(ROWS, D)], 1)(own_text, other_text, back1, back2)
-    i2 = along_x(i2, 2)
+    (grad_text,) = call(sum_kernel, 4, [f32(ROWS, D)], 60)(own_text, other_text, back1, back2)
+    (i1,) = call(add_kernel, 2, [f32(ROWS, D)], 0)(i1, along_x(i2, -1))
     i1 = along_x(i1, -1)
     i3 = along_x(i3, 1)
 
@@ -318,12 +322,12 @@
         pl.pallas_call(
             final_kernel,
             grid=(1,),
-            in_specs=[pl.BlockSpec((8, 128), lambda i: (0, 0))] + [first] * 7,
+            in_specs=[pl.BlockSpec((8, 128), lambda i: (0, 0))] + [first] * 6,
             out_specs=[first] * 2,
             out_shape=[f32(ROWS, D)] * 2,
             compiler_params=pltpu.CompilerParams(vmem_limit_bytes=VMEM_LIMIT),
             name="finish",
-        )(scalars, images, captions, grad_text, i0, i2, i1, i3)
+        )(scalars, images, captions, i0, i1, i3, grad_text)
     )
 
 

time: 75.4 us -> 74.7 us (level)
  the two profiles are of different devices: /device:TPU:1 before, /device:TPU:67 now
where the time goes in v5:
time: 74.7 us; the launch traced here: 74.2 us
  starting transfers between devices  39.6 us (53%)
  waiting for transfers between devices  23.2 us (31%)
  Pallas kernels  8.1 us (11%)
  between operations  2.25 us (3%)
  local copies, waits for them, and re-layouts  1.05 us (1%)
    ppermute x4, waiting for transfers between devices, along_loop(): lax.ppermute(shard, 'loop', [(i, (i + by) % count) for i in range(count)])  23.2 us
    ppermute x6, starting transfers between devices, along_x(): return lax.ppermute(shard, 'group', pairs)  17 us
    ppermute x4, starting transfers between devices, along_loop(): lax.ppermute(shard, 'loop', [(i, (i + by) % count) for i in range(count)])  16.7 us
    ppermute x2, starting transfers between devices, across_cores(): return lax.ppermute(shard, 'group', [(i, i ^ 1) for i in range(count)])  5.91 us
    pallas_call x1, Pallas kernels, per_device(): call(own_kernel, 7, image_halves + [f32(8, images_all)] + weight_halves +...  2.13 us
    pallas_call x1, Pallas kernels, per_device(): call(cross_kernel, 5, text_halves + weight_halves + [f32(texts_all, D)], 2)  1.97 us
  transfers between devices with their start and end apart: 12, of which 3 were waited for; matrix products, arithmetic and copies ran while one was open for 0% of the time, Pallas kernels for 7%

profile of v5, /device:TPU:67, one launch (start us, length us, event | category | flops | bytes accessed | tf_op | source)
XLA Modules:
  0.0 74.2 jit_solution(1148354402275600291)
XLA Ops:
  0.6 0.0 copy-start.3
  0.6 4.0 %collective-permute-start = (f32[64,1152]{1,0:T(8,128)}, f32[64,1152]{1,0:T(8,128)S(1)}, u32[]{:S(2)}, u32[]{:S(2)}) collective-permute-start(f32[64,1152]{1,0:T(8,128)} %captions.1), channel_id=1, source_target_pairs={{0,8},{8,16},{16,24},{24,32},{32,40},{40,48},{48,56},{56,64},{64,7... | collective-permute-start | bytes 884744 | tf_op jit(solution)/shard_map/ppermute | solution.py:19
  4.6 0.0 copy-done.3
  4.7 0.0 copy-start
  4.7 1.0 %copy-done = f32[64,1152]{1,0:T(8,128)S(1)} copy-done((f32[64,1152]{1,0:T(8,128)S(1)}, f32[64,1152]{1,0:T(8,128)}, u32[]{:S(2)}) %copy-start) | copy-done | bytes 294936
  5.6 0.2 pack_kernel.1.p0
  5.8 2.2 %collective-permute-start.1 = (f32[72,1152]{1,0:T(8,128)S(1)}, f32[72,1152]{1,0:T(8,128)S(1)}, u32[]{:S(2)}, u32[]{:S(2)}) collective-permute-start(f32[72,1152]{1,0:T(8,128)S(1)} %pack_kernel.1.p0), channel_id=1, source_target_pairs={{0,2},{1,7},{2,4},{3,1},{4,6},{5,3},{6,0},{7,5},{8,10},{9,15},{10,... | collective-permute-start | bytes 995336 | tf_op jit(solution)/shard_map/ppermute | solution.py:25
  8.0 3.1 %collective-permute-start.3 = (f32[72,1152]{1,0:T(8,128)S(1)}, f32[72,1152]{1,0:T(8,128)S(1)}, u32[]{:S(2)}, u32[]{:S(2)}) collective-permute-start(f32[72,1152]{1,0:T(8,128)S(1)} %pack_kernel.1.p0), channel_id=1, source_target_pairs={{0,6},{1,3},{2,0},{3,5},{4,2},{5,7},{6,4},{7,1},{8,14},{9,11},{10,... | collective-permute-start | bytes 995336 | tf_op jit(solution)/shard_map/ppermute | solution.py:25
  12.4 0.1 stack.27.places
  12.5 0.0 copy-start.2
  12.5 0.0 collective-permute-done.text
  12.5 0.1 unit_kernel.1.u1
  12.6 4.0 %collective-permute-start.4 = (f32[64,1152]{1,0:T(8,128)S(1)}, f32[64,1152]{1,0:T(8,128)S(1)}, u32[]{:S(2)}, u32[]{:S(2)}) collective-permute-start(f32[64,1152]{1,0:T(8,128)S(1)} %unit_kernel.1.u1), channel_id=1, source_target_pairs={{0,8},{8,16},{16,24},{24,32},{32,40},{40,48},{48,56},{56,64},{64,7... | collective-permute-start | bytes 884744 | tf_op jit(solution)/shard_map/ppermute | solution.py:19
  16.7 0.0 collective-permute-done.1.p1
  16.7 3.2 %collective-permute-start.2 = (f32[72,1152]{1,0:T(8,128)S(1)}, f32[72,1152]{1,0:T(8,128)S(1)}, u32[]{:S(2)}, u32[]{:S(2)}) collective-permute-start(f32[72,1152]{1,0:T(8,128)S(1)} %collective-permute-done.1.p1), channel_id=1, source_target_pairs={{0,2},{1,7},{2,4},{3,1},{4,6},{5,3},{6,0},{7,5},{8,10},{9,15},{10,... | collective-permute-start | bytes 995336 | tf_op jit(solution)/shard_map/ppermute | solution.py:25
  19.9 0.0 copy-done.2
  19.9 1.1 %early_kernel.1 = (f32[8,128]{1,0:T(8,128)S(1)}, f32[128,1152]{1,0:T(8,128)S(1)}, bf16[128,1152]{1,0:T(8,128)(2,1)S(1)}, bf16[128,1152]{1,0:T(8,128)(2,1)S(1)}) custom-call(f32[1]{0:T(128)S(6)} %copy.7.log_scale, f32[1]{0:T(128)S(6)} %copy.8.logit_bias, s32[6]{0:T(128)S(1)} %stack.27.places, f32[64,1152]{1,0:T(8,128)S(1)} %copy-done.2, ...), custom_call_target="tpu_custom_call" | custom-call | flops 20384317440 | bytes 7077888 | tf_op jit(solution)/shard_map/early_kernel/pallas_call | solution.py:274
  21.0 11.3 %collective-permute-done.4.u2 = f32[64,1152]{1,0:T(8,128)S(1)} collective-permute-done((f32[64,1152]{1,0:T(8,128)S(1)}, f32[64,1152]{1,0:T(8,128)S(1)}, u32[]{:S(2)}, u32[]{:S(2)}) %collective-permute-start.4) | collective-permute-done | bytes 294944 | tf_op jit(solution)/shard_map/ppermute | solution.py:19
  32.3 0.1 late_kernel.1
  32.4 3.8 %collective-permute-start.5 = (f32[192,1152]{1,0:T(8,128)S(1)}, f32[192,1152]{1,0:T(8,128)S(1)}, u32[]{:S(2)}, u32[]{:S(2)}) collective-permute-start(f32[192,1152]{1,0:T(8,128)S(1)} %get-tuple-element.34), channel_id=1, source_target_pairs={{0,1},{1,0},{2,3},{3,2},{4,5},{5,4},{6,7},{7,6},{8,9},{9,8},{10,11... | collective-permute-start | bytes 2654216 | tf_op jit(solution)/shard_map/ppermute | solution.py:30
  36.2 0.0 collective-permute-done.3.p3
  36.2 0.0 collective-permute-done.2.p2
  36.2 2.1 %own_kernel.1 = (bf16[256,1152]{1,0:T(8,128)(2,1)S(1)}, bf16[256,1152]{1,0:T(8,128)(2,1)S(1)}, f32[8,256]{1,0:T(8,128)S(1)}, bf16[192,256]{1,0:T(8,128)(2,1)S(1)...) custom-call(f32[8,128]{1,0:T(8,128)S(1)} %get-tuple-element.26.scalars, f32[72,1152]{1,0:T(8,128)S(1)} %pack_kernel.1.p0, ...), custom_call_target="tpu_custom_call" | custom-call | flops 20384317440 | bytes 7077888 | tf_op jit(solution)/shard_map/own_kernel/pallas_call | solution.py:292
  38.4 0.0 collective-permute-done.5.units
  38.4 2.0 %cross_kernel.1 = (bf16[192,1152]{1,0:T(8,128)(2,1)S(1)}, bf16[192,1152]{1,0:T(8,128)(2,1)S(1)}, bf16[192,256]{1,0:T(8,128)(2,1)S(1)}, bf16[192,256]{1,0:T(8,128)(2,1)S(1)}, f32[192,1152]{1,0:T(8,128)S(1)}) custom-call(f32[8,128]{1,0:T(8,128)S(1)} %get-tuple-element.26.scalars, f32[192,1152]{1,0:T(8,128)S(1)} %collective-permute-done.5.units, ...), custom_call_target="tpu_custom_call" | custom-call | flops 679477248 | bytes 7077888 | tf_op jit(solution)/shard_map/cross_kernel/pallas_call | solution.py:298
  40.4 2.1 %collective-permute-start.9 = (f32[192,1152]{1,0:T(8,128)S(1)}, f32[192,1152]{1,0:T(8,128)S(1)}, u32[]{:S(2)}, u32[]{:S(2)}) collective-permute-start(f32[192,1152]{1,0:T(8,128)S(1)} %get-tuple-element.47), channel_id=1, source_target_pairs={{0,1},{1,0},{2,3},{3,2},{4,5},{5,4},{6,7},{7,6},{8,9},{9,8},{10,11... | collective-permute-start | bytes 2654216 | tf_op jit(solution)/shard_map/ppermute | solution.py:30
  42.5 1.2 %image_kernel.1 = (f32[64,1152]{1,0:T(8,128)S(1)}, f32[64,1152]{1,0:T(8,128)S(1)}, f32[64,1152]{1,0:T(8,128)S(1)}, f32[64,1152]{1,0:T(8,128)S(1)}) custom-call(bf16[192,256]{1,0:T(8,128)(2,1)S(1)} %get-tuple-element.32.w_high, bf16[192,256]{1,0:T(8,128)(2,1)S(1)} %get-tuple-element.33.w_low, bf16[192,1152]{1,0:T(8,128)(2,1)S(1)} %get-tuple-element.30.t_high, ...), custom_call_target="tpu_custom_call" | custom-call | flops 679477248 | bytes 7077888 | tf_op jit(solution)/shard_map/image_kernel/pallas_call | solution.py:302
  43.7 3.1 %collective-permute-start.6 = (f32[64,1152]{1,0:T(8,128)S(1)}, f32[64,1152]{1,0:T(8,128)S(1)}, u32[]{:S(2)}, u32[]{:S(2)}) collective-permute-start(f32[64,1152]{1,0:T(8,128)S(1)} %get-tuple-element.44), channel_id=1, source_target_pairs={{0,6},{1,3},{2,0},{3,5},{4,2},{5,7},{6,4},{7,1},{8,14},{9,11},{10,... | collective-permute-start | bytes 884744 | tf_op jit(solution)/shard_map/ppermute | solution.py:25
  46.9 0.0 collective-permute-done.9.other
  46.9 0.1 last_kernel.1
  46.9 6.7 %collective-permute-start.10 = (f32[64,1152]{1,0:T(8,128)S(1)}, f32[64,1152]{1,0:T(8,128)S(1)}, u32[]{:S(2)}, u32[]{:S(2)}) collective-permute-start(f32[64,1152]{1,0:T(8,128)S(1)} %get-tuple-element.48), channel_id=1, source_target_pairs={{0,760},{8,0},{16,8},{24,16},{32,24},{40,32},{48,40},{56,48},{64,5... | collective-permute-start | bytes 884744 | tf_op jit(solution)/shard_map/ppermute | solution.py:19
  53.6 2.0 %collective-permute-start.11 = (f32[64,1152]{1,0:T(8,128)S(1)}, f32[64,1152]{1,0:T(8,128)S(1)}, u32[]{:S(2)}, u32[]{:S(2)}) collective-permute-start(f32[64,1152]{1,0:T(8,128)S(1)} %get-tuple-element.49), channel_id=1, source_target_pairs={{0,752},{8,760},{16,0},{24,8},{32,16},{40,24},{48,32},{56,40},{64,... | collective-permute-start | bytes 884744 | tf_op jit(solution)/shard_map/ppermute | solution.py:19
  55.7 2.1 %collective-permute-start.8 = (f32[64,1152]{1,0:T(8,128)S(1)}, f32[64,1152]{1,0:T(8,128)S(1)}, u32[]{:S(2)}, u32[]{:S(2)}) collective-permute-start(f32[64,1152]{1,0:T(8,128)S(1)} %get-tuple-element.45), channel_id=1, source_target_pairs={{0,2},{1,7},{2,4},{3,1},{4,6},{5,3},{6,0},{7,5},{8,10},{9,15},{10,... | collective-permute-start | bytes 884744 | tf_op jit(solution)/shard_map/ppermute | solution.py:25
  57.7 0.0 collective-permute-done.6.b
  57.8 0.0 copy-start.1
  57.8 3.4 %collective-permute-start.7 = (f32[64,1152]{1,0:T(8,128)S(1)}, f32[64,1152]{1,0:T(8,128)S(1)}, u32[]{:S(2)}, u32[]{:S(2)}) collective-permute-start(f32[64,1152]{1,0:T(8,128)S(1)} %add_kernel.1), channel_id=1, source_target_pairs={{0,6},{1,3},{2,0},{3,5},{4,2},{5,7},{6,4},{7,1},{8,14},{9,11},{10,... | collective-permute-start | bytes 884744 | tf_op jit(solution)/shard_map/ppermute | solution.py:25
  61.2 1.1 %collective-permute-done.10.back1 = f32[64,1152]{1,0:T(8,128)S(1)} collective-permute-done((f32[64,1152]{1,0:T(8,128)S(1)}, f32[64,1152]{1,0:T(8,128)S(1)}, u32[]{:S(2)}, u32[]{:S(2)}) %collective-permute-start.10) | collective-permute-done | bytes 294944 | tf_op jit(solution)/shard_map/ppermute | solution.py:19
  62.3 10.8 %collective-permute-done.11.back2 = f32[64,1152]{1,0:T(8,128)S(1)} collective-permute-done((f32[64,1152]{1,0:T(8,128)S(1)}, f32[64,1152]{1,0:T(8,128)S(1)}, u32[]{:S(2)}, u32[]{:S(2)}) %collective-permute-start.11) | collective-permute-done | bytes 294944 | tf_op jit(solution)/shard_map/ppermute | solution.py:19
  73.1 0.1 sum_kernel.1.grad_text
  73.1 0.0 collective-permute-done.8.i3
  73.2 0.0 collective-permute-done.7.i1
  73.2 0.0 copy-done.1
  73.2 1.1 %finish.1 = (f32[64,1152]{1,0:T(8,128)}, f32[64,1152]{1,0:T(8,128)}) custom-call(f32[8,128]{1,0:T(8,128)S(1)} %get-tuple-element.26.scalars, f32[64,1152]{1,0:T(8,128)S(1)} %copy-done.1, f32[64,1152]{1,0:T(8,128)S(1)} %copy-done.2, f32[64,1152]{1,0:T(8,128)S(1)} %get-tuple-element.42.after.i0, f32[64,1152]{1,0:T(8,128)S(1)} %collective-permute-done.7.i1, ...), custom_call_target="tpu_custom_call" | custom-call | tf_op jit(solution)/shard_map/finish/pallas_call | solution.py:322
  (1 shorter events, 0.0 us)
Async XLA Ops:
  0.6 4.0 %copy-start.3 = (s32[64]{0:T(128)S(1)}, s32[64]{0:T(128)}, u32[]{:S(2)}) copy-start(s32[64]{0:T(128)} %param.7) | copy-start | bytes 772
  0.6 11.9 %collective-permute-start = (f32[64,1152]{1,0:T(8,128)}, f32[64,1152]{1,0:T(8,128)S(1)}, u32[]{:S(2)}, u32[]{:S(2)}) collective-permute-start(f32[64,1152]{1,0:T(8,128)} %captions.1), channel_id=1, source_target_pairs={{0,8},{8,16},{16,24},{24,32},{32,40},{40,48},{48,56},{56,64},{64,7... | collective-permute-start | bytes 884744 | tf_op jit(solution)/shard_map/ppermute | solution.py:19
  4.7 1.0 %copy-start = (f32[64,1152]{1,0:T(8,128)S(1)}, f32[64,1152]{1,0:T(8,128)}, u32[]{:S(2)}) copy-start(f32[64,1152]{1,0:T(8,128)} %images.3) | copy-start | bytes 884740
  5.8 10.9 %collective-permute-start.1 = (f32[72,1152]{1,0:T(8,128)S(1)}, f32[72,1152]{1,0:T(8,128)S(1)}, u32[]{:S(2)}, u32[]{:S(2)}) collective-permute-start(f32[72,1152]{1,0:T(8,128)S(1)} %pack_kernel.1.p0), channel_id=1, source_target_pairs={{0,2},{1,7},{2,4},{3,1},{4,6},{5,3},{6,0},{7,5},{8,10},{9,15},{10,... | collective-permute-start | bytes 995336 | tf_op jit(solution)/shard_map/ppermute | solution.py:25
  8.0 28.3 %collective-permute-start.3 = (f32[72,1152]{1,0:T(8,128)S(1)}, f32[72,1152]{1,0:T(8,128)S(1)}, u32[]{:S(2)}, u32[]{:S(2)}) collective-permute-start(f32[72,1152]{1,0:T(8,128)S(1)} %pack_kernel.1.p0), channel_id=1, source_target_pairs={{0,6},{1,3},{2,0},{3,5},{4,2},{5,7},{6,4},{7,1},{8,14},{9,11},{10,... | collective-permute-start | bytes 995336 | tf_op jit(solution)/shard_map/ppermute | solution.py:25
  12.5 7.3 %copy-start.2 = (f32[64,1152]{1,0:T(8,128)S(1)}, f32[64,1152]{1,0:T(8,128)}, u32[]{:S(2)}) copy-start(f32[64,1152]{1,0:T(8,128)} %captions.1) | copy-start | bytes 884740
  12.6 19.6 %collective-permute-start.4 = (f32[64,1152]{1,0:T(8,128)S(1)}, f32[64,1152]{1,0:T(8,128)S(1)}, u32[]{:S(2)}, u32[]{:S(2)}) collective-permute-start(f32[64,1152]{1,0:T(8,128)S(1)} %unit_kernel.1.u1), channel_id=1, source_target_pairs={{0,8},{8,16},{16,24},{24,32},{32,40},{40,48},{48,56},{56,64},{64,7... | collective-permute-start | bytes 884744 | tf_op jit(solution)/shard_map/ppermute | solution.py:19
  16.7 19.6 %collective-permute-start.2 = (f32[72,1152]{1,0:T(8,128)S(1)}, f32[72,1152]{1,0:T(8,128)S(1)}, u32[]{:S(2)}, u32[]{:S(2)}) collective-permute-start(f32[72,1152]{1,0:T(8,128)S(1)} %collective-permute-done.1.p1), channel_id=1, source_target_pairs={{0,2},{1,7},{2,4},{3,1},{4,6},{5,3},{6,0},{7,5},{8,10},{9,15},{10,... | collective-permute-start | bytes 995336 | tf_op jit(solution)/shard_map/ppermute | solution.py:25
  32.4 5.9 %collective-permute-start.5 = (f32[192,1152]{1,0:T(8,128)S(1)}, f32[192,1152]{1,0:T(8,128)S(1)}, u32[]{:S(2)}, u32[]{:S(2)}) collective-permute-start(f32[192,1152]{1,0:T(8,128)S(1)} %get-tuple-element.34), channel_id=1, source_target_pairs={{0,1},{1,0},{2,3},{3,2},{4,5},{5,4},{6,7},{7,6},{8,9},{9,8},{10,11... | collective-permute-start | bytes 2654216 | tf_op jit(solution)/shard_map/ppermute | solution.py:30
  40.4 6.5 %collective-permute-start.9 = (f32[192,1152]{1,0:T(8,128)S(1)}, f32[192,1152]{1,0:T(8,128)S(1)}, u32[]{:S(2)}, u32[]{:S(2)}) collective-permute-start(f32[192,1152]{1,0:T(8,128)S(1)} %get-tuple-element.47), channel_id=1, source_target_pairs={{0,1},{1,0},{2,3},{3,2},{4,5},{5,4},{6,7},{7,6},{8,9},{9,8},{10,11... | collective-permute-start | bytes 2654216 | tf_op jit(solution)/shard_map/ppermute | solution.py:30
  43.7 14.0 %collective-permute-start.6 = (f32[64,1152]{1,0:T(8,128)S(1)}, f32[64,1152]{1,0:T(8,128)S(1)}, u32[]{:S(2)}, u32[]{:S(2)}) collective-permute-start(f32[64,1152]{1,0:T(8,128)S(1)} %get-tuple-element.44), channel_id=1, source_target_pairs={{0,6},{1,3},{2,0},{3,5},{4,2},{5,7},{6,4},{7,1},{8,14},{9,11},{10,... | collective-permute-start | bytes 884744 | tf_op jit(solution)/shard_map/ppermute | solution.py:25
  46.9 15.3 %collective-permute-start.10 = (f32[64,1152]{1,0:T(8,128)S(1)}, f32[64,1152]{1,0:T(8,128)S(1)}, u32[]{:S(2)}, u32[]{:S(2)}) collective-permute-start(f32[64,1152]{1,0:T(8,128)S(1)} %get-tuple-element.48), channel_id=1, source_target_pairs={{0,760},{8,0},{16,8},{24,16},{32,24},{40,32},{48,40},{56,48},{64,5... | collective-permute-start | bytes 884744 | tf_op jit(solution)/shard_map/ppermute | solution.py:19
  53.6 19.4 %collective-permute-start.11 = (f32[64,1152]{1,0:T(8,128)S(1)}, f32[64,1152]{1,0:T(8,128)S(1)}, u32[]{:S(2)}, u32[]{:S(2)}) collective-permute-start(f32[64,1152]{1,0:T(8,128)S(1)} %get-tuple-element.49), channel_id=1, source_target_pairs={{0,752},{8,760},{16,0},{24,8},{32,16},{40,24},{48,32},{56,40},{64,... | collective-permute-start | bytes 884744 | tf_op jit(solution)/shard_map/ppermute | solution.py:19
  55.7 17.5 %collective-permute-start.8 = (f32[64,1152]{1,0:T(8,128)S(1)}, f32[64,1152]{1,0:T(8,128)S(1)}, u32[]{:S(2)}, u32[]{:S(2)}) collective-permute-start(f32[64,1152]{1,0:T(8,128)S(1)} %get-tuple-element.45), channel_id=1, source_target_pairs={{0,2},{1,7},{2,4},{3,1},{4,6},{5,3},{6,0},{7,5},{8,10},{9,15},{10,... | collective-permute-start | bytes 884744 | tf_op jit(solution)/shard_map/ppermute | solution.py:25
  57.8 15.4 %copy-start.1 = (f32[64,1152]{1,0:T(8,128)S(1)}, f32[64,1152]{1,0:T(8,128)}, u32[]{:S(2)}) copy-start(f32[64,1152]{1,0:T(8,128)} %images.3) | copy-start | bytes 884740
  57.8 15.4 %collective-permute-start.7 = (f32[64,1152]{1,0:T(8,128)S(1)}, f32[64,1152]{1,0:T(8,128)S(1)}, u32[]{:S(2)}, u32[]{:S(2)}) collective-permute-start(f32[64,1152]{1,0:T(8,128)S(1)} %add_kernel.1), channel_id=1, source_target_pairs={{0,6},{1,3},{2,0},{3,5},{4,2},{5,7},{6,4},{7,1},{8,14},{9,11},{10,... | collective-permute-start | bytes 884744 | tf_op jit(solution)/shard_map/ppermute | solution.py:25
